TPU v7x, 32 devices: a whole 2x2x4 slice. The times are simulated.
32 devices in a mesh: rep: 4 (over y, x), shard: 8 (over z, core).
Axes of the slice: x: 2, y: 2, z: 4, core: 2. Of those that a mesh axis runs over, the one named last changes fastest.
Arguments:
- tokens: bfloat16 [32768, 768], P(('rep', 'shard')), may hold values from -6 to 6
- cotangent: bfloat16 [32768, 768], P(('rep', 'shard')), may hold values from -6 to 6
- task: int32 [256], P(('rep', 'shard')), may hold values from 0 to 2
- lengths: int32 [256], P(('rep', 'shard')), may hold values from 64 to 128
- task_masks: int32 [3, 32768], P(None, ('rep', 'shard')), may hold values 0 or 1
- w_qkv: bfloat16 [768, 2304], P('shard'), may hold values from -0.21875 to 0.21875
- qv_bias: bfloat16 [1536], P('shard'), may hold values from -3 to 3
- w_out: bfloat16 [768, 768], P('shard'), may hold values from -0.625 to 0.625
- out_bias: bfloat16 [768], P('shard'), may hold values from -3 to 3
- ln1_gain: bfloat16 [768], P('shard'), may hold values from 0.5 to 1.5
- ln1_bias: bfloat16 [768], P('shard'), may hold values from -3 to 3
- w_up: bfloat16 [768, 3072], P('shard'), may hold values from -0.21875 to 0.21875
- up_bias: bfloat16 [3072], P('shard'), may hold values from -3 to 3
- w_down: bfloat16 [3072, 768], P('shard'), may hold values from -0.109375 to 0.109375
- down_bias: bfloat16 [768], P('shard'), may hold values from -3 to 3
- ln2_gain: bfloat16 [768], P('shard'), may hold values from 0.5 to 1.5
- ln2_bias: bfloat16 [768], P('shard'), may hold values from -3 to 3
Outputs:
- output: bfloat16 [32768, 768], P(('rep', 'shard'))
- grad_tokens: bfloat16 [32768, 768], P(('rep', 'shard'))
- grad_w_qkv: float32 [768, 2304], P('shard')
- grad_qv_bias: float32 [1536], P('shard')
- grad_w_out: float32 [768, 768], P('shard')
- grad_out_bias: float32 [768], P('shard')
- grad_ln1_gain: float32 [768], P('shard')
- grad_ln1_bias: float32 [768], P('shard')
- grad_w_up: float32 [768, 3072], P('shard')
- grad_up_bias: float32 [3072], P('shard')
- grad_w_down: float32 [3072, 768], P('shard')
- grad_down_bias: float32 [768], P('shard')
- grad_ln2_gain: float32 [768], P('shard')
- grad_ln2_bias: float32 [768], P('shard')
Inputs may be any that keep to these rules, and one draw needn't show every extreme that they name: `task`: 0 masked language, 1 masked region, 2 image-text matching.
All inputs are finite; a program needn't handle non-finite values. No bound on the sum of `task_masks` on one device may be relied on, other than what follows from the above.
Results may differ from a plain program's by a relative error of at most 0.015.
Values may be sent and summed in bfloat16 or wider, within the bound.
No kernel may reach another device: no remote copies, remote signals or barrier semaphores. Data moves between devices by JAX's collectives and lax.ppermute only.
A program may use at most 192 MiB of HBM per device.

v0:
```python
import jax
import jax.numpy as jnp
from jax import lax
from jax.sharding import PartitionSpec as P

HD = 64
LEN = 128


EPSILON = 1e-06


def exact_gelu(values_in):
    return jax.nn.gelu(values_in, approximate=False)


def normalize(summed, gain, shift):
    centre = jnp.mean(summed, -1, keepdims=True)
    deviation = summed - centre
    variance = jnp.mean(deviation * deviation, -1, keepdims=True)
    rscale = lax.rsqrt(variance + EPSILON)
    normed = deviation * rscale
    return (normed * gain.astype(jnp.float32) + shift.astype(jnp.float32), normed, rscale)


def norm_back(grad_norm, normed, rscale):
    first_mean = jnp.mean(grad_norm, -1, keepdims=True)
    second_mean = jnp.mean(grad_norm * normed, -1, keepdims=True)
    return rscale * (grad_norm - first_mean - normed * second_mean)


def row_sums(gradient_low):
    return jnp.sum(gradient_low.astype(jnp.float32), 0)


def per_device(
    tokens,
    cotangent,
    task,
    lengths,
    task_masks,
    w_qkv,
    qv_bias,
    w_out,
    out_bias,
    ln1_gain,
    ln1_bias,
    w_up,
    up_bias,
    w_down,
    down_bias,
    ln2_gain,
    ln2_bias,
):
    gathered = (
        lax.all_gather(w_qkv, "shard", axis=0, tiled=True),
        lax.all_gather(qv_bias, "shard", axis=0, tiled=True),
        lax.all_gather(w_out, "shard", axis=0, tiled=True),
        lax.all_gather(out_bias, "shard", axis=0, tiled=True),
        lax.all_gather(ln1_gain, "shard", axis=0, tiled=True),
        lax.all_gather(ln1_bias, "shard", axis=0, tiled=True),
        lax.all_gather(w_up, "shard", axis=0, tiled=True),
        lax.all_gather(up_bias, "shard", axis=0, tiled=True),
        lax.all_gather(w_down, "shard", axis=0, tiled=True),
        lax.all_gather(down_bias, "shard", axis=0, tiled=True),
        lax.all_gather(ln2_gain, "shard", axis=0, tiled=True),
        lax.all_gather(ln2_bias, "shard", axis=0, tiled=True),
    )
    (
        qkv_weight,
        qv_shift,
        out_weight,
        out_shift,
        gain_one,
        shift_one,
        up_weight,
        up_shift,
        down_weight,
        down_shift,
        gain_two,
        shift_two,
    ) = gathered
    row_count, model_width = tokens.shape
    seq_count = task.shape[0]
    head_count = model_width // HD
    inputs = tokens.astype(jnp.float32)
    position = jnp.arange(LEN, dtype=jnp.int32)
    key_valid = position[None, :] < lengths[:, None]
    zero_shift = jnp.zeros((model_width,), jnp.float32)
    qv_float = qv_shift.astype(jnp.float32)
    qkv_shift = jnp.concatenate([qv_float[:model_width], zero_shift, qv_float[model_width:]])
    projected = (
        jnp.dot(tokens, qkv_weight, preferred_element_type=jnp.float32) + qkv_shift
    ).astype(jnp.bfloat16)
    packed = projected.reshape(seq_count, LEN, 3, head_count, HD)
    queries = packed[:, :, 0]
    key_rows = packed[:, :, 1]
    value_rows = packed[:, :, 2]

    def masked_scores():
        scores = (
            jnp.einsum("sqhe,skhe->shqk", queries, key_rows, preferred_element_type=jnp.float32)
            * 0.125
        )
        return jnp.where(key_valid[:, None, None, :], scores, -1000000000.0)

    masked = masked_scores()
    row_max = jnp.max(masked, -1, keepdims=True)
    exponent = jnp.exp(masked - row_max)
    row_total = jnp.sum(exponent, -1, keepdims=True)
    attention = exponent / row_total
    log_total = row_max + jnp.log(row_total)
    attention_low = attention.astype(jnp.bfloat16)
    context = jnp.einsum(
        "shqk,skhe->sqhe", attention_low, value_rows, preferred_element_type=jnp.float32
    )
    context = context.reshape(row_count, model_width).astype(jnp.bfloat16)
    attended = jnp.dot(context, out_weight, preferred_element_type=jnp.float32) + out_shift.astype(
        jnp.float32
    )
    first_norm, norm_one, scale_one = normalize(inputs + attended, gain_one, shift_one)
    first_low = first_norm.astype(jnp.bfloat16)
    inner = jnp.dot(first_low, up_weight, preferred_element_type=jnp.float32) + up_shift.astype(
        jnp.float32
    )
    activated = exact_gelu(inner).astype(jnp.bfloat16)
    ffn_out = jnp.dot(
        activated, down_weight, preferred_element_type=jnp.float32
    ) + down_shift.astype(jnp.float32)
    output, norm_two, scale_two = normalize(first_norm + ffn_out, gain_two, shift_two)
    result = output.astype(jnp.bfloat16)
    regathered = (
        lax.all_gather(w_qkv, "shard", axis=0, tiled=True),
        lax.all_gather(qv_bias, "shard", axis=0, tiled=True),
        lax.all_gather(w_out, "shard", axis=0, tiled=True),
        lax.all_gather(out_bias, "shard", axis=0, tiled=True),
        lax.all_gather(ln1_gain, "shard", axis=0, tiled=True),
        lax.all_gather(ln1_bias, "shard", axis=0, tiled=True),
        lax.all_gather(w_up, "shard", axis=0, tiled=True),
        lax.all_gather(up_bias, "shard", axis=0, tiled=True),
        lax.all_gather(w_down, "shard", axis=0, tiled=True),
        lax.all_gather(down_bias, "shard", axis=0, tiled=True),
        lax.all_gather(ln2_gain, "shard", axis=0, tiled=True),
        lax.all_gather(ln2_bias, "shard", axis=0, tiled=True),
    )
    (
        qkv_weight,
        qv_shift,
        out_weight,
        out_shift,
        gain_one,
        shift_one,
        up_weight,
        up_shift,
        down_weight,
        down_shift,
        gain_two,
        shift_two,
    ) = regathered
    token_task = jnp.repeat(task, LEN)
    chosen = jnp.where(
        token_task == 0, task_masks[0], jnp.where(token_task == 1, task_masks[1], task_masks[2])
    )
    row_weight = (chosen * key_valid.reshape(row_count).astype(jnp.int32)).astype(jnp.float32)
    grad_output = cotangent.astype(jnp.float32) * row_weight[:, None]
    grad_gain_two = jnp.sum(grad_output * norm_two, 0)
    grad_shift_two = jnp.sum(grad_output, 0)
    grad_middle = norm_back(grad_output * gain_two.astype(jnp.float32), norm_two, scale_two)
    ffn_grad = grad_middle.astype(jnp.bfloat16)
    grad_down = jnp.einsum("rf,rd->fd", activated, ffn_grad, preferred_element_type=jnp.float32)
    grad_down_shift = row_sums(ffn_grad)
    grad_active = jnp.einsum("rd,fd->rf", ffn_grad, down_weight, preferred_element_type=jnp.float32)
    unused_value, gelu_back = jax.vjp(exact_gelu, inner)
    inner_grad = gelu_back(grad_active)[0].astype(jnp.bfloat16)
    grad_up = jnp.einsum("rd,rf->df", first_low, inner_grad, preferred_element_type=jnp.float32)
    grad_up_shift = row_sums(inner_grad)
    grad_first = grad_middle + jnp.einsum(
        "rf,df->rd", inner_grad, up_weight, preferred_element_type=jnp.float32
    )
    grad_gain_one = jnp.sum(grad_first * norm_one, 0)
    grad_shift_one = jnp.sum(grad_first, 0)
    grad_summed = norm_back(grad_first * gain_one.astype(jnp.float32), norm_one, scale_one)
    attend_grad = grad_summed.astype(jnp.bfloat16)
    grad_out_weight = jnp.einsum(
        "rc,rd->cd", context, attend_grad, preferred_element_type=jnp.float32
    )
    grad_out_shift = row_sums(attend_grad)
    context_grad = jnp.einsum(
        "rd,cd->rc", attend_grad, out_weight, preferred_element_type=jnp.float32
    )
    context_grad = context_grad.astype(jnp.bfloat16).reshape(seq_count, LEN, head_count, HD)
    recomputed = jnp.exp(masked_scores() - log_total)
    recomputed_low = recomputed.astype(jnp.bfloat16)
    grad_values = jnp.einsum(
        "shqk,sqhe->skhe", recomputed_low, context_grad, preferred_element_type=jnp.float32
    )
    grad_attention = jnp.einsum(
        "sqhe,skhe->shqk", context_grad, value_rows, preferred_element_type=jnp.float32
    )
    inner_sum = jnp.sum(recomputed * grad_attention, -1, keepdims=True)
    grad_scores = (recomputed * (grad_attention - inner_sum)).astype(jnp.bfloat16)
    grad_queries = (
        jnp.einsum("shqk,skhe->sqhe", grad_scores, key_rows, preferred_element_type=jnp.float32)
        * 0.125
    )
    grad_keys = (
        jnp.einsum("shqk,sqhe->skhe", grad_scores, queries, preferred_element_type=jnp.float32)
        * 0.125
    )
    grad_packed = jnp.stack([grad_queries, grad_keys, grad_values], axis=2)
    grad_packed = grad_packed.reshape(row_count, 3 * model_width).astype(jnp.bfloat16)
    grad_qkv = jnp.einsum("rd,re->de", tokens, grad_packed, preferred_element_type=jnp.float32)
    packed_sums = row_sums(grad_packed)
    grad_qv_shift = jnp.concatenate([packed_sums[:model_width], packed_sums[2 * model_width :]])
    grad_input = (
        grad_summed
        + jnp.einsum("re,de->rd", grad_packed, qkv_weight, preferred_element_type=jnp.float32)
    ).astype(jnp.bfloat16)
    shared = (
        lax.psum_scatter(grad_qkv, "shard", scatter_dimension=0, tiled=True),
        lax.psum_scatter(grad_qv_shift, "shard", scatter_dimension=0, tiled=True),
        lax.psum_scatter(grad_out_weight, "shard", scatter_dimension=0, tiled=True),
        lax.psum_scatter(grad_out_shift, "shard", scatter_dimension=0, tiled=True),
        lax.psum_scatter(grad_gain_one, "shard", scatter_dimension=0, tiled=True),
        lax.psum_scatter(grad_shift_one, "shard", scatter_dimension=0, tiled=True),
        lax.psum_scatter(grad_up, "shard", scatter_dimension=0, tiled=True),
        lax.psum_scatter(grad_up_shift, "shard", scatter_dimension=0, tiled=True),
        lax.psum_scatter(grad_down, "shard", scatter_dimension=0, tiled=True),
        lax.psum_scatter(grad_down_shift, "shard", scatter_dimension=0, tiled=True),
        lax.psum_scatter(grad_gain_two, "shard", scatter_dimension=0, tiled=True),
        lax.psum_scatter(grad_shift_two, "shard", scatter_dimension=0, tiled=True),
    )
    final = (
        lax.psum(shared[0].astype(jnp.bfloat16), "rep").astype(jnp.float32),
        lax.psum(shared[1].astype(jnp.bfloat16), "rep").astype(jnp.float32),
        lax.psum(shared[2].astype(jnp.bfloat16), "rep").astype(jnp.float32),
        lax.psum(shared[3].astype(jnp.bfloat16), "rep").astype(jnp.float32),
        lax.psum(shared[4].astype(jnp.bfloat16), "rep").astype(jnp.float32),
        lax.psum(shared[5].astype(jnp.bfloat16), "rep").astype(jnp.float32),
        lax.psum(shared[6].astype(jnp.bfloat16), "rep").astype(jnp.float32),
        lax.psum(shared[7].astype(jnp.bfloat16), "rep").astype(jnp.float32),
        lax.psum(shared[8].astype(jnp.bfloat16), "rep").astype(jnp.float32),
        lax.psum(shared[9].astype(jnp.bfloat16), "rep").astype(jnp.float32),
        lax.psum(shared[10].astype(jnp.bfloat16), "rep").astype(jnp.float32),
        lax.psum(shared[11].astype(jnp.bfloat16), "rep").astype(jnp.float32),
    )
    (
        final_qkv,
        final_qv,
        final_out,
        final_out_shift,
        final_gain_one,
        final_shift_one,
        final_up,
        final_up_shift,
        final_down,
        final_down_shift,
        final_gain_two,
        final_shift_two,
    ) = final
    return (
        result,
        grad_input,
        final_qkv,
        final_qv,
        final_out,
        final_out_shift,
        final_gain_one,
        final_shift_one,
        final_up,
        final_up_shift,
        final_down,
        final_down_shift,
        final_gain_two,
        final_shift_two,
    )


def solution(mesh):
    in_specs = (
        P(("rep", "shard"), None),
        P(("rep", "shard"), None),
        P(("rep", "shard")),
        P(("rep", "shard")),
        P(None, ("rep", "shard")),
        P("shard", None),
        P("shard"),
        P("shard", None),
        P("shard"),
        P("shard"),
        P("shard"),
        P("shard", None),
        P("shard"),
        P("shard", None),
        P("shard"),
        P("shard"),
        P("shard"),
    )
    out_specs = (
        P(("rep", "shard"), None),
        P(("rep", "shard"), None),
        P("shard", None),
        P("shard"),
        P("shard", None),
        P("shard"),
        P("shard"),
        P("shard"),
        P("shard", None),
        P("shard"),
        P("shard", None),
        P("shard"),
        P("shard"),
        P("shard"),
    )
    return jax.shard_map(
        per_device, mesh=mesh, in_specs=in_specs, out_specs=out_specs, check_vma=False
    )
```

profile of v0, /device:TPU:0, one launch (start us, length us, event | category | flops | bytes accessed | tf_op | source)
XLA Modules:
  0.0 639.7 jit_solution(14184570292638677903)
XLA Ops:
  20.6 31.6 %all-reduce.16 = (bf16[1536]{0:T(1024)(128)(2,1)S(1)}, bf16[768]{0:T(1024)(128)(2,1)S(1)}, bf16[768]{0:T(1024)(128)(2,1)S(1)}, bf16[768]{0:T(1024)(128)(2,1)S(1)...) all-reduce(bf16[1536]{0:T(1024)(128)(2,1)S(1)} %dynamic-update-slic, ...), channel_id=1, replica_groups=mesh['rep'=4,'shard'=8] {'shard'}, use_global_device_ids=true, to_apply=%add | all-reduce | flops 6144 | bytes 24576
  52.3 12.7 %all-gather = bf16[8,1,384]{2,1,0:T(2,128)(2,1)S(1)} all-gather(bf16[1,1,384]{2,1,0:T(2,128)(2,1)S(1)} %reshape.183), channel_id=1, replica_groups=mesh['rep'=4,'shard'=8] {'shard'}, dimensions={0}, use_global_device_ids=true | all-gather | bytes 6912 | tf_op jit(solution)/shard_map/all_gather | solution.py:63
  65.8 1.7 copy.77
  67.6 1.6 copy.69
  69.3 7.4 %add_convert_fusion.1 = bf16[1024,2304]{1,0:T(8,128)(2,1)} fusion(bf16[1024,768]{1,0:T(8,128)(2,1)S(1)} %copy-done.12, bf16[768,2304]{1,0:T(8,128)(2,1)} %all-gather.6.cloned.1.call-done, f32[2304]{0:T(1024)S(1)} %pad_maximum_fusion), kind=kOutput, calls=%fused_computation.20 | convolution fusion | flops 3628597248 | bytes 9839616 | tf_op jit(solution)/shard_map/dot_general | solution.py:93
  76.7 6.7 %copy.70 = bf16[1024,2304]{0,1:T(8,128)(2,1)} copy(bf16[1024,2304]{1,0:T(8,128)(2,1)} %add_convert_fusion.1) | data formatting | bytes 9437184 | tf_op jit(solution)/shard_map/convert_element_type | solution.py:94
  83.4 3.6 copy.102
  87.5 2.2 fusion.50
  89.7 1.6 fusion.6
  94.9 4.0 fusion.51
  99.0 1.7 copy-done.1
  101.0 29.9 %all-gather.10.cloned.1.call-done = bf16[768,3072]{1,0:T(8,128)(2,1)} async-done(((bf16[96,3072]{1,0:T(8,128)(2,1)}), bf16[768,3072]{1,0:T(8,128)(2,1)}) %all-gather.10.cloned.1.call-update) | async-done | bytes 4718608 | tf_op jit(solution)/shard_map/all_gather | solution.py:62
  130.9 38.0 %multiply_convert_fusion = (bf16[1024,3072]{1,0:T(8,128)(2,1)}, f32[1024,3072]{1,0:T(8,128)}, f32[1024,3072]{1,0:T(8,128)}) fusion(f32[3072]{0:T(1024)S(1)} %bitcast.112, bf16[768,3072]{1,0:T(8,128)(2,1)} %all-gather.10.cloned.1.call-done, f32[1024,768]{0,1:T(8,128)} %copy-done.1, f32[768]{0:T(1024)S(1)} %convert_element_type.186, ...), kind=kOutput, calls=%fused_computation.4 | convolution fusion | flops 5043388416 | bytes 39348224 | tf_op jit(solution)/shard_map/dot_general | solution.py:123
  168.9 14.0 %all-gather.12.cloned.1.call-done = bf16[3072,768]{1,0:T(8,128)(2,1)} async-done(((bf16[384,768]{1,0:T(8,128)(2,1)}), bf16[3072,768]{1,0:T(8,128)(2,1)}) %all-gather.12.cloned.1.call-update) | async-done | bytes 4718608 | tf_op jit(solution)/shard_map/all_gather | solution.py:64
  183.0 9.8 %fusion.52 = (f32[1024]{0:T(1024)S(1)}, f32[1024,768]{0,1:T(8,128)S(1)}) fusion(f32[768]{0:T(1024)S(1)} %convert_element_type.190, bf16[1024,3072]{1,0:T(8,128)(2,1)} %get-tuple-element.97, bf16[3072,768]{1,0:T(8,128)(2,1)} %all-gather.12.cloned.1.call-done, f32[768]{0:T(1024)S(1)} %convert_element_type.186, f32[768]{0:T(1024)S(1)} %convert_element_type.185, ...), kind=kOutput, calls=%fused_computation.114 | convolution fusion | flops 4837342208 | bytes 17323008 | tf_op jit(solution)/shard_map/dot_general | solution.py:127
  194.7 2.7 convert_reduce_fusion.2
  197.4 17.5 %convert_reduce_fusion = (f32[3072]{0:T(1024)S(1)}, bf16[1024,3072]{1,0:T(8,128)(2,1)}) fusion(f32[1024,3072]{1,0:T(8,128)} %get-tuple-element.98, bf16[1024,768]{0,1:T(8,128)(2,1)S(1)} %get-tuple-element.92, bf16[3072,768]{1,0:T(8,128)(2,1)} %all-gather.12.cloned.1.call-done, f32[1024,3072]{1,0:T(8,128)} %get-tuple-element.118, f32[3072]{0:T(1024)S(1)} %bitcast.113), kind=kOutput, calls=%fused_computation.2 | convolution fusion | flops 4885312512 | bytes 37773312 | tf_op jit(solution)/shard_map/rd,fd->rf/dot_general | solution.py:172
  214.9 11.2 %multiply_reduce_fusion.2 = (f32[768]{0:T(1024)S(1)}, f32[1024]{0:T(1024)S(1)}, f32[1024]{0:T(1024)S(1)}, f32[768]{0:T(1024)S(1)}, f32[1024,768]{0,1:T(8,128)S(1)}) fusion(f32[1024,768]{0,1:T(8,128)} %copy-done.1, f32[1024]{0:T(1024)S(1)} %add_rsqrt_fusion.1, f32[1024]{0:T(1024)S(1)} %broadcast_multiply_fusion.5, f32[768]{0:T(1024)S(1)} %convert_element_type.185, ...), kind=kOutput, calls=%fused_computation.38 | convolution fusion | flops 4846776320 | bytes 22069248 | tf_op jit(solution)/shard_map/rf,df->rd/dot_general | solution.py:177
  227.6 2.8 fusion.27
  230.5 3.9 convolution_convert_fusion
  234.4 1.9 copy.79
  236.8 4.8 multiply_reduce_fusion
  241.7 2.2 multiply_convert_fusion.1
  243.9 3.8 multiply_bitcast_fusion
  248.6 2.3 fusion.21
  250.9 1.9 convert_reduce_fusion.1
  252.8 9.3 %copy.85 = bf16[8,128,3,12,64]{1,0,4,3,2:T(8,128)(2,1)S(1)} copy(bf16[8,128,3,12,64]{1,4,3,0,2:T(8,128)(2,1)S(1)} %get-tuple-element.96) | data formatting | bytes 9437184 | tf_op jit(solution)/shard_map/convert_element_type | solution.py:211
  262.1 2.1 copy-done.10
  264.2 5.8 convolution_bitcast_fusion
  270.0 8.0 %copy.97 = f32[768,2304]{1,0:T(8,128)} copy(f32[768,2304]{0,1:T(8,128)} %convolution_bitcast_fusion) | data formatting | bytes 14155776
  278.1 1.8 copy-done.3
  279.9 10.8 %fusion.39 = f32[768,3072]{1,0:T(8,128)} fusion(bf16[1024,3072]{1,0:T(8,128)(2,1)} %get-tuple-element.125, f32[1024,768]{0,1:T(8,128)S(1)} %copy-done.3, f32[768]{0:T(1024)S(1)} %convert_element_type.186, f32[768]{0:T(1024)S(1)} %convert_element_type.185, f32[1024]{0:T(1024)S(1)} %add_rsqrt_fusion.1, f32[1024]{0:T(1024)S(1)} %broadcast_multiply_fusion.5), kind=kOutput, calls=%fused_computation.105 | convolution fusion | flops 4835770368 | bytes 18888704 | tf_op jit(solution)/shard_map/rd,rf->df/dot_general | solution.py:175
  292.1 10.2 %fusion.53 = f32[3072,768]{1,0:T(8,128)} fusion(bf16[1024,3072]{1,0:T(8,128)(2,1)} %get-tuple-element.97, bf16[1024,768]{0,1:T(8,128)(2,1)S(1)} %copy-done.17), kind=kOutput, calls=%fused_computation.115 | convolution fusion | flops 4831838208 | bytes 17301504 | tf_op jit(solution)/shard_map/rf,rd->fd/dot_general | solution.py:170
  302.5 1.6 convert_element_type.210
  304.1 50.2 %reduce-scatter.13.cloned.1.call-done = f32[96,2304]{1,0:T(8,128)} async-done(((f32[768,2304]{1,0:T(8,128)}), f32[96,2304]{1,0:T(8,128)}) %reduce-scatter.13.cloned.1.call-update) | async-done | bytes 884752
  354.3 2.2 copy.98
  356.5 98.0 %reduce-scatter.9.cloned.1.call-done = f32[96,3072]{1,0:T(8,128)} async-done(((f32[768,3072]{1,0:T(8,128)}), f32[96,3072]{1,0:T(8,128)}) %reduce-scatter.9.cloned.1.call-update) | async-done | bytes 1179664 | tf_op jit(solution)/shard_map/reduce_scatter | solution.py:226
  454.5 2.2 convert_element_type.219
  456.6 98.0 %reduce-scatter.11.cloned.1.call-done = f32[384,768]{1,0:T(8,128)} async-done(((f32[3072,768]{1,0:T(8,128)}), f32[384,768]{1,0:T(8,128)}) %reduce-scatter.11.cloned.1.call-update) | async-done | bytes 1179664 | tf_op jit(solution)/shard_map/reduce_scatter | solution.py:228
  554.7 2.1 convert_element_type.224
  558.8 1.6 copy.87
  560.5 26.4 %all-reduce.15 = (bf16[1536]{0:T(1024)(128)(2,1)S(1)}, bf16[768]{0:T(1024)(128)(2,1)S(1)}, bf16[768]{0:T(1024)(128)(2,1)S(1)}, bf16[768]{0:T(1024)(128)(2,1)S(1)...) all-reduce(f32[1536]{0:T(1024)S(1)} %pad_maximum_fusion.1, ...), channel_id=3, replica_groups=mesh['rep'=4,'shard'=8] {'shard'}, use_global_device_ids=true, to_apply=%region_14.15.clone | all-reduce | flops 9216 | bytes 55296
  587.6 10.0 %all-reduce.17 = (bf16[192]{0:T(256)(128)(2,1)S(1)}, bf16[96]{0:T(256)(128)(2,1)S(1)}, bf16[96]{0:T(256)(128)(2,1)S(1)}, bf16[96]{0:T(256)(128)(2,1)S(1)}, bf16[...) all-reduce(bf16[192]{0:T(256)(128)(2,1)S(1)} %dynamic-slice.32, ...), channel_id=1, replica_groups=mesh['rep'=4,'shard'=8] {'rep'}, use_global_device_ids=true, to_apply=%region_15.16 | all-reduce | flops 1152 | bytes 4608 | tf_op jit(solution)/shard_map/psum | solution.py:235
  601.8 8.1 %add_convert_fusion.2 = bf16[1024,768]{0,1:T(8,128)(2,1)S(1)} fusion(f32[1024,768]{0,1:T(8,128)} %copy-done.11, bf16[768,2304]{1,0:T(8,128)(2,1)} %all-gather.6.cloned.1.call-done, bf16[288,8,8,128]{3,2,1,0:T(8,128)(2,1)} %bitcast.106), kind=kOutput, calls=%fused_computation.40 | convolution fusion | flops 3625451520 | bytes 12976128 | tf_op jit(solution)/shard_map/re,de->rd/dot_general | solution.py:217
  611.5 14.0 %all-reduce.21.cloned.1.call-done = (bf16[96,2304]{0,1:T(8,128)(2,1)}, bf16[96,768]{1,0:T(8,128)(2,1)}, bf16[96,3072]{1,0:T(8,128)(2,1)}, bf16[384,768]{1,0:T(8,128)(2,1)}) async-done(((bf16[96,2304]{0,1:T(8,128)(2,1)}, bf16[96,768]{1,0:T(8,128)(2,1)}, bf16[96,3072]{1,0:T(8,128)(2,1)}, bf16[384,768]{1,0:T(8,128)(2,1)}), (bf16[96,2304]{0,1:T(8,128)(2,1)}, bf16[96,768]{1,0:T(8,128)(2,1)}, ...) | async-done | bytes 1769488 | tf_op jit(solution)/shard_map/psum | solution.py:234
  625.5 2.3 copy.89
  627.8 1.6 convert_element_type.211
  629.4 2.2 convert_element_type.220
  (140 shorter events, 31.4 us)
Async XLA Ops:
  7.2 60.4 %copy-start.12 = (bf16[1024,768]{1,0:T(8,128)(2,1)S(1)}, bf16[1024,768]{1,0:T(8,128)(2,1)}, u32[]{:S(2)}) copy-start(bf16[1024,768]{1,0:T(8,128)(2,1)} %param.17) | copy-start | bytes 4718596
  7.2 62.1 %all-gather.6.cloned.1.call-start = ((), (), s32[]{:S(2)}) async-start(), calls=%async_computation.4 | async-start | bytes 3981312 | tf_op jit(solution)/shard_map/all_gather | solution.py:56
  7.9 87.0 %all-gather.8.cloned.1.call-start = ((), (), s32[]{:S(2)}) async-start(), calls=%async_computation.5 | async-start | bytes 1327104 | tf_op jit(solution)/shard_map/all_gather | solution.py:58
  8.7 122.2 %all-gather.10.cloned.1.call-start = ((), (), s32[]{:S(2)}) async-start(), calls=%async_computation.6 | async-start | bytes 5308416 | tf_op jit(solution)/shard_map/all_gather | solution.py:62
  9.4 173.5 %all-gather.12.cloned.1.call-start = ((), (), s32[]{:S(2)}) async-start(), calls=%async_computation.7 | async-start | bytes 5308416 | tf_op jit(solution)/shard_map/all_gather | solution.py:64
  10.0 292.5 %reduce-scatter.7.cloned.1.call-start = ((), (), s32[]{:S(2)}) async-start(), calls=%async_computation.8 | async-start | bytes 2654208 | tf_op jit(solution)/shard_map/reduce_scatter | solution.py:222
  65.8 3.4 copy-start.23
  87.4 2.2 copy-start.4
  87.5 2.2 copy-start.6
  87.5 3.9 copy-start.8
  89.7 2.6 copy-start
  89.7 2.7 copy-start.19
  91.3 2.3 copy-start.21
  94.9 4.1 copy-start.14
  99.0 1.7 copy-start.1
  197.4 17.5 %copy-start.16 = (bf16[1024,768]{0,1:T(8,128)(2,1)}, bf16[1024,768]{0,1:T(8,128)(2,1)S(1)}, u32[]{:S(2)}) copy-start(bf16[1024,768]{0,1:T(8,128)(2,1)S(1)} %get-tuple-element.92) | copy-start | bytes 4718596
  214.9 11.2 %copy-start.2 = (f32[1024,768]{0,1:T(8,128)S(1)}, f32[1024,768]{0,1:T(8,128)}, u32[]{:S(2)}) copy-start(f32[1024,768]{0,1:T(8,128)} %copy-done.1) | copy-start | bytes 9437188
  226.2 1.4 copy-start.15
  227.3 3.2 copy-start.11
  227.6 2.9 copy-start.20
  227.6 2.9 copy-start.22
  230.4 123.8 %reduce-scatter.13.cloned.1.call-start = ((), (), s32[]{:S(2)}) async-start(), calls=%async_computation.11 | async-start | bytes 7962624
  234.4 2.4 copy-start.9
  236.8 4.9 slice-start
  236.8 4.9 slice-start.1
  243.9 3.8 copy-start.5
  252.8 11.4 %copy-start.13 = (bf16[1024,768]{1,0:T(8,128)(2,1)S(1)}, bf16[1024,768]{1,0:T(8,128)(2,1)}, u32[]{:S(2)}) copy-start(bf16[1024,768]{1,0:T(8,128)(2,1)} %param.17) | copy-start | bytes 4718596
  262.1 2.1 copy-start.10
  278.0 1.9 copy-start.3
  278.1 176.4 %reduce-scatter.9.cloned.1.call-start = ((), (), s32[]{:S(2)}) async-start(), calls=%async_computation.9 | async-start | bytes 10616832 | tf_op jit(solution)/shard_map/reduce_scatter | solution.py:226
  290.7 1.4 copy-start.17
  290.7 263.9 %reduce-scatter.11.cloned.1.call-start = ((), (), s32[]{:S(2)}) async-start(), calls=%async_computation.10 | async-start | bytes 10616832 | tf_op jit(solution)/shard_map/reduce_scatter | solution.py:228
  302.4 323.1 %all-reduce.21.cloned.1.call-start = ((), (), s32[]{:S(2)}) async-start(), calls=%async_computation.12 | async-start | bytes 3833856 | tf_op jit(solution)/shard_map/psum | solution.py:234
  304.1 254.7 %copy-start.7 = (bf16[1024,768]{0,1:T(8,128)(2,1)S(1)}, bf16[1024,768]{0,1:T(8,128)(2,1)}, u32[]{:S(2)}) copy-start(bf16[1024,768]{0,1:T(8,128)(2,1)} %get-tuple-element.102) | copy-start | bytes 4718596
  625.5 6.1 copy-start.18
Sparse Core Ops, SparseCore 0:
  9.7 44.8 all-gather.5
  56.2 21.5 all-gather.7
  79.4 51.4 all-gather.9
  132.4 50.5 all-gather.11
  230.5 35.0 reduce-scatter.6
  278.2 76.0 reduce-scatter.12
  356.6 97.8 reduce-scatter.8
  456.8 97.8 reduce-scatter.10
  559.3 66.1 all-reduce.20
where the time goes:
time: 651 us; the launch traced here: 640 us
  waiting for transfers between devices  307 us (47%)
  matrix products  145 us (22%)
  blocking collectives  80.7 us (12%)
  local copies, waits for them, and re-layouts  60.4 us (9%)
  other arithmetic  28.4 us (4%)
  between operations  18.1 us (3%)
    reduce_scatter x1, waiting for transfers between devices, per_device(): lax.psum_scatter(grad_down, 'shard', scatter_dimension=0, tiled=True)  98 us
    reduce_scatter x1, waiting for transfers between devices, per_device(): lax.psum_scatter(grad_up, 'shard', scatter_dimension=0, tiled=True)  98 us
    unnamed x2, blocking collectives  58 us
    unnamed x10, waiting for transfers between devices  52.8 us
    unnamed x85, local copies, waits for them, and re-layouts  39.8 us
    dot_general x1, matrix products, per_device(): jnp.dot(first_low, up_weight, preferred_element_type=jnp.float32)  38 us
    all_gather x1, waiting for transfers between devices, per_device(): lax.all_gather(w_up, 'shard', axis=0, tiled=True)  29.9 us
    dot_general x1, matrix products, per_device(): jnp.einsum('rd,fd->rf', ffn_grad, down_weight, preferred_element_type=jnp...  17.5 us
  transfers between devices with their start and end apart: 9, of which 6 were waited for; matrix products, arithmetic and copies ran while one was open for 26% of the time, Pallas kernels for 0%

commit v1 on v0

v1 whole, which is shorter than its diff:
```python
import functools

import jax
import jax.numpy as jnp
from jax import lax
from jax.experimental import pallas as pl
from jax.experimental.pallas import tpu as pltpu
from jax.sharding import PartitionSpec as P

HD = 64
LEN = 128
EPSILON = 1e-06
BF = jnp.bfloat16
F32 = jnp.float32
MIB = 1024 * 1024

TAIL_P = 0.36
TAIL = (0.143717436, 0.141710663, 0.140057471, 0.0256236997, 0.182297768, -0.180751783, 0.0473446063)
DENSITY = 0.3989422804014327


def dot_nn(left, right):
    return jnp.dot(left, right, preferred_element_type=F32)


def dot_nt(left, right):
    return lax.dot_general(left, right, (((1,), (1,)), ((), ())), preferred_element_type=F32)


def dot_tn(left, right):
    return lax.dot_general(left, right, (((0,), (0,)), ((), ())), preferred_element_type=F32)


def gelu_parts(inner):
    size = jnp.abs(inner)
    t = 1.0 / (1.0 + TAIL_P * size)
    bell = jnp.exp(-0.5 * inner * inner)
    poly = TAIL[6]
    for coefficient in TAIL[5::-1]:
        poly = poly * t + coefficient
    tail = poly * t * bell
    phi = jnp.where(inner < 0, tail, 1.0 - tail)
    return inner * phi, phi + inner * (bell * DENSITY)


def norm_parts(summed):
    centre = jnp.mean(summed, -1, keepdims=True)
    deviation = summed - centre
    variance = jnp.mean(deviation * deviation, -1, keepdims=True)
    rscale = lax.rsqrt(variance + EPSILON)
    return deviation * rscale, rscale


def norm_back(grad_norm, normed, rscale):
    first_mean = jnp.mean(grad_norm, -1, keepdims=True)
    second_mean = jnp.mean(grad_norm * normed, -1, keepdims=True)
    return rscale * (grad_norm - first_mean - normed * second_mean)


def add_rows(total_ref, rows):
    @pl.when(pl.program_id(0) == 0)
    def _():
        total_ref[...] = jnp.zeros_like(total_ref)

    for at, values in enumerate(rows):
        total_ref[at : at + 1, :] += jnp.sum(values, 0, keepdims=True)


def cost(flops, moved):
    return pl.CostEstimate(flops=int(flops), bytes_accessed=int(moved), transcendentals=0)


def params(vmem=48):
    return pltpu.CompilerParams(vmem_limit_bytes=vmem * MIB)


def whole(shape):
    return pl.BlockSpec(shape, lambda i, *_: (0,) * len(shape))


def rows_of(block, width):
    return pl.BlockSpec((block, width), lambda i, *_: (i, 0))


def head_masks():
    lane = lax.broadcasted_iota(jnp.int32, (1, 2 * HD), 1)
    return (lane < HD).astype(BF), (lane >= HD).astype(BF)


def stack_heads(pair, masks):
    return jnp.concatenate([pair * masks[0], pair * masks[1]], axis=0)


def attention_forward_kernel(plan, place, lengths, x_ref, shift_ref, *refs):
    pieces, (proj_ref, ctx_ref, lse_ref, w_ref), sems = refs[: len(plan)], refs[len(plan) : len(plan) + 4], refs[len(plan) + 4]
    block, width = x_ref.shape
    step = pl.program_id(0)

    @pl.when(step == 0)
    def _():
        bring(plan, place, pieces, w_ref, sems)

    x = x_ref[...]
    for unit in range(3):
        at = slice(unit * width, (unit + 1) * width)
        proj_ref[:, at] = (dot_nn(x, w_ref[unit]) + shift_ref[:, at]).astype(BF)
    masks = head_masks()
    lane = lax.broadcasted_iota(jnp.int32, (1, LEN), 1)
    for seq in range(block // LEN):
        rows = slice(seq * LEN, (seq + 1) * LEN)
        valid = lane < lengths[step * (block // LEN) + seq]
        lse = jnp.zeros((LEN, LEN), F32)
        for pair in range(width // (2 * HD)):
            at = pair * 2 * HD
            q = proj_ref[rows, at : at + 2 * HD] * BF(0.125)
            k = proj_ref[rows, width + at : width + at + 2 * HD]
            v = proj_ref[rows, 2 * width + at : 2 * width + at + 2 * HD]
            scores = dot_nt(q, stack_heads(k, masks))
            probs = []
            for half in range(2):
                masked = jnp.where(valid, scores[:, half * LEN : (half + 1) * LEN], -1e9)
                top = jnp.max(masked, -1, keepdims=True)
                exponent = jnp.exp(masked - top)
                total = jnp.sum(exponent, -1, keepdims=True)
                probs.append((exponent * (1.0 / total)).astype(BF))
                lse = jnp.where(lane == 2 * pair + half, top + jnp.log(total), lse)
            ctx = dot_nn(jnp.concatenate(probs, axis=1), stack_heads(v, masks))
            ctx_ref[rows, at : at + 2 * HD] = ctx.astype(BF)
        lse_ref[seq] = lse.T[: lse_ref.shape[1]]


def bring(plan, place, pieces, w_ref, sems):
    rep, chip, core = place[0], place[1], place[2]
    copies = []
    for piece, entries in zip(pieces, plan):
        for at, (unit, flip, other, ahead, first, count, depth) in enumerate(entries):
            to_unit = (rep ^ unit) if flip else unit
            shard = 2 * ((chip + ahead) % 4) + (core ^ other)
            row = pl.multiple_of(shard * depth + first, 16)
            copies.append(pltpu.make_async_copy(piece.at[at], w_ref.at[to_unit, pl.ds(row, count)], sems.at[len(copies)]))
    for copy in copies:
        copy.start()
    for copy in copies:
        copy.wait()


def weight_args(weight, shape):
    plan, pieces = weight
    return plan, pieces, [pl.BlockSpec(memory_space=pl.ANY)] * len(pieces), pltpu.SemaphoreType.DMA((sum(len(p) for p in plan),))


def attention_forward(place, lengths, tokens, shift, weight):
    rows, width = tokens.shape
    block = 2 * LEN
    heads = width // HD
    lse_rows = -(-heads // 8) * 8
    plan, pieces, specs, sems = weight_args(weight, None)
    return pl.pallas_call(
        functools.partial(attention_forward_kernel, plan),
        grid_spec=pltpu.PrefetchScalarGridSpec(
            num_scalar_prefetch=2,
            grid=(rows // block,),
            in_specs=[rows_of(block, width), whole((1, 3 * width))] + specs,
            out_specs=[
                rows_of(block, 3 * width),
                rows_of(block, width),
                pl.BlockSpec((block // LEN, lse_rows, LEN), lambda i, *_: (i, 0, 0)),
                whole((4, width, width)),
            ],
            scratch_shapes=[sems],
        ),
        out_shape=[
            jax.ShapeDtypeStruct((rows, 3 * width), BF),
            jax.ShapeDtypeStruct((rows, width), BF),
            jax.ShapeDtypeStruct((rows // LEN, lse_rows, LEN), F32),
            jax.ShapeDtypeStruct((4, width, width), BF),
        ],
        compiler_params=params(),
        cost_estimate=cost(6 * rows * width * width * 2, 14e6),
        name="attention_forward",
    )(place, lengths, tokens, shift, *pieces)


def middle_kernel(plan, place, x_ref, ctx_ref, w_out_ref, vec_ref, up_shift_ref, *refs):
    pieces = refs[: len(plan)]
    norm_ref, scale_ref, low_ref, act_ref, slope_ref, w_ref, sems = refs[len(plan) :]
    width = x_ref.shape[1]

    @pl.when(pl.program_id(0) == 0)
    def _():
        bring(plan, place, pieces, w_ref, sems)

    attended = dot_nn(ctx_ref[...], w_out_ref[0]) + vec_ref[0:1, :]
    normed, rscale = norm_parts(x_ref[...].astype(F32) + attended)
    norm_ref[...] = normed
    scale_ref[...] = rscale
    low = (normed * vec_ref[1:2, :] + vec_ref[2:3, :]).astype(BF)
    low_ref[...] = low
    for unit in range(w_ref.shape[0]):
        at = slice(unit * width, (unit + 1) * width)
        act, slope = gelu_parts(dot_nn(low, w_ref[unit]) + up_shift_ref[:, at])
        act_ref[:, at] = act.astype(BF)
        slope_ref[:, at] = slope.astype(BF)


def middle(place, tokens, context, w_qkvo, vecs, up_shift, weight, block=256):
    rows, width = tokens.shape
    hidden = up_shift.shape[1]
    units = hidden // width
    plan, pieces, specs, sems = weight_args(weight, None)
    return pl.pallas_call(
        functools.partial(middle_kernel, plan),
        grid_spec=pltpu.PrefetchScalarGridSpec(
            num_scalar_prefetch=1,
            grid=(rows // block,),
            in_specs=[
                rows_of(block, width),
                rows_of(block, width),
                pl.BlockSpec((1, width, width), lambda i, *_: (3, 0, 0)),
                whole(vecs.shape),
                whole(up_shift.shape),
            ]
            + specs,
            out_specs=[
                rows_of(block, width),
                rows_of(block, 1),
                rows_of(block, width),
                rows_of(block, hidden),
                rows_of(block, hidden),
                whole((units, width, width)),
            ],
            scratch_shapes=[sems],
        ),
        out_shape=[
            jax.ShapeDtypeStruct((rows, width), F32),
            jax.ShapeDtypeStruct((rows, 1), F32),
            jax.ShapeDtypeStruct((rows, width), BF),
            jax.ShapeDtypeStruct((rows, hidden), BF),
            jax.ShapeDtypeStruct((rows, hidden), BF),
            jax.ShapeDtypeStruct((units, width, width), BF),
        ],
        compiler_params=params(),
        cost_estimate=cost(2 * rows * width * (width + hidden), 25e6),
        name="middle",
    )(place, tokens, context, w_qkvo, vecs, up_shift, *pieces)


def ffn_out_kernel(act_ref, w_ref, norm_ref, cot_ref, weight_ref, vec_ref, out_ref, dz_ref, low_ref, sum_ref):
    first = norm_ref[...] * vec_ref[1:2, :] + vec_ref[2:3, :]
    normed, rscale = norm_parts(first + (dot_nn(act_ref[...], w_ref[...]) + vec_ref[3:4, :]))
    out_ref[...] = (normed * vec_ref[4:5, :] + vec_ref[5:6, :]).astype(BF)
    grad = cot_ref[...].astype(F32) * weight_ref[...]
    dz = norm_back(grad * vec_ref[4:5, :], normed, rscale)
    low = dz.astype(BF)
    dz_ref[...] = dz
    low_ref[...] = low
    add_rows(sum_ref, (grad * normed, grad, low.astype(F32)))


def ffn_out(act, w_down, norm_one, cotangent, row_weight, vecs, block=256):
    rows, width = cotangent.shape
    hidden = act.shape[1]
    return pl.pallas_call(
        ffn_out_kernel,
        grid=(rows // block,),
        in_specs=[
            rows_of(block, hidden),
            whole((hidden, width)),
            rows_of(block, width),
            rows_of(block, width),
            rows_of(block, 1),
            whole(vecs.shape),
        ],
        out_specs=[rows_of(block, width), rows_of(block, width), rows_of(block, width), whole((8, width))],
        out_shape=[
            jax.ShapeDtypeStruct((rows, width), BF),
            jax.ShapeDtypeStruct((rows, width), F32),
            jax.ShapeDtypeStruct((rows, width), BF),
            jax.ShapeDtypeStruct((8, width), F32),
        ],
        compiler_params=params(),
        cost_estimate=cost(2 * rows * width * hidden, 22e6),
        name="ffn_out",
    )(act, w_down, norm_one, cotangent, row_weight, vecs)


def grad_down_kernel(low_ref, act_ref, out_ref, turned_ref):
    @pl.when(pl.program_id(0) == 0)
    def _():
        turned_ref[...] = low_ref[...].T

    grad = dot_nn(turned_ref[...], act_ref[...])
    part = out_ref.shape[2]
    for at in range(out_ref.shape[0]):
        out_ref[at] = grad[:, at * part : (at + 1) * part].astype(BF)


def grad_down_natural(low, act, shards, span=768):
    rows, width = low.shape
    hidden = act.shape[1]
    part = hidden // shards
    each = max(1, span // part)
    return pl.pallas_call(
        grad_down_kernel,
        grid=(shards // each,),
        in_specs=[whole((rows, width)), pl.BlockSpec((rows, each * part), lambda i: (0, i))],
        out_specs=pl.BlockSpec((each, width, part), lambda i: (i, 0, 0)),
        out_shape=jax.ShapeDtypeStruct((shards, width, part), BF),
        scratch_shapes=[pltpu.VMEM((width, rows), BF)],
        compiler_params=params(),
        cost_estimate=cost(2 * rows * width * hidden, 13e6),
        name="grad_down",
    )(low, act)


def inner_grad_kernel(low_ref, w_ref, slope_ref, out_ref, sum_ref):
    width = low_ref.shape[1]

    @pl.when(pl.program_id(0) == 0)
    def _():
        sum_ref[...] = jnp.zeros_like(sum_ref)

    for unit in range(w_ref.shape[0] // width):
        at = slice(unit * width, (unit + 1) * width)
        grad = (dot_nt(low_ref[...], w_ref[at, :]) * slope_ref[:, at].astype(F32)).astype(BF)
        out_ref[:, at] = grad
        sum_ref[0:1, at] += jnp.sum(grad.astype(F32), 0, keepdims=True)


def inner_grad(low, w_down, slope, block=256):
    rows, width = low.shape
    hidden = slope.shape[1]
    return pl.pallas_call(
        inner_grad_kernel,
        grid=(rows // block,),
        in_specs=[rows_of(block, width), whole((hidden, width)), rows_of(block, hidden)],
        out_specs=[rows_of(block, hidden), whole((8, hidden))],
        out_shape=[jax.ShapeDtypeStruct((rows, hidden), BF), jax.ShapeDtypeStruct((8, hidden), F32)],
        compiler_params=params(),
        cost_estimate=cost(2 * rows * width * hidden, 18e6),
        name="inner_grad",
    )(low, w_down, slope)


def unit_grads_kernel(sources, relative, place, *refs):
    lefts, (right_ref, tail_ref) = refs[:sources], refs[sources : sources + 2]
    outs, (turned_ref, grad_ref) = refs[sources + 2 : -2], refs[-2:]
    step = pl.program_id(0)

    @pl.when(step == 0)
    def _():
        turned_ref[...] = lefts[0][...].T

    if sources == 2:

        @pl.when(step == 3)
        def _():
            turned_ref[...] = lefts[1][...].T
            grad_ref[...] = dot_nn(turned_ref[...], tail_ref[...]).astype(BF)

        @pl.when(step < 3)
        def _():
            grad_ref[...] = dot_nn(turned_ref[...], right_ref[...]).astype(BF)
    else:
        grad_ref[...] = dot_nn(turned_ref[...], right_ref[...]).astype(BF)
    if not relative:
        outs[0][0] = grad_ref[...]
        return
    chip, core = place[1], place[2]
    depth = outs[0].shape[2]
    for other in range(4):
        ahead = (other - chip) % 4
        for out, which in zip(outs, (core, 1 - core)):
            row = pl.multiple_of((2 * other + which) * depth, 16)
            out[0, ahead] = grad_ref[pl.ds(row, depth), :]


def unit_grads(place, lefts, right, tail, relative):
    rows, width = lefts[0].shape
    last = right.shape[1] // width - 1
    if relative:
        depth = width // 8
        out_specs = [pl.BlockSpec((1, 4, depth, width), lambda i, place: (i ^ place[0], 0, 0, 0))] * 2
        out_shape = [jax.ShapeDtypeStruct((4, 4, depth, width), BF)] * 2
    else:
        out_specs = [pl.BlockSpec((1, width, width), lambda i, place: (i, 0, 0))]
        out_shape = [jax.ShapeDtypeStruct((4, width, width), BF)]
    return pl.pallas_call(
        functools.partial(unit_grads_kernel, len(lefts), relative),
        grid_spec=pltpu.PrefetchScalarGridSpec(
            num_scalar_prefetch=1,
            grid=(4,),
            in_specs=[whole((rows, width))] * len(lefts)
            + [pl.BlockSpec((rows, width), lambda i, place: (0, jnp.minimum(i, last))), whole((rows, width))],
            out_specs=out_specs,
            scratch_shapes=[pltpu.VMEM((width, rows), BF), pltpu.VMEM((width, width), BF)],
        ),
        out_shape=out_shape,
        compiler_params=params(),
        cost_estimate=cost(2 * rows * width * width * 4, 13e6),
        name="unit_grads",
    )(place, *lefts, right, tail)


def first_grad_kernel(inner_ref, w_ref, dz_ref, norm_ref, scale_ref, vec_ref, w_out_ref, out_ref, low_ref, ctx_ref, sum_ref):
    width = dz_ref.shape[1]
    grad = dz_ref[...]
    for unit in range(w_ref.shape[0]):
        grad += dot_nt(inner_ref[:, unit * width : (unit + 1) * width], w_ref[unit])
    normed = norm_ref[...]
    summed = norm_back(grad * vec_ref[1:2, :], normed, scale_ref[...])
    out_ref[...] = summed
    low = summed.astype(BF)
    low_ref[...] = low
    ctx_ref[...] = dot_nt(low, w_out_ref[0]).astype(BF)
    add_rows(sum_ref, (grad * normed, grad, low.astype(F32)))


def first_grad(inner, w_up, dz, norm_one, scale_one, vecs, w_qkvo, block=256):
    rows, width = dz.shape
    hidden = inner.shape[1]
    return pl.pallas_call(
        first_grad_kernel,
        grid=(rows // block,),
        in_specs=[
            rows_of(block, hidden),
            whole(w_up.shape),
            rows_of(block, width),
            rows_of(block, width),
            rows_of(block, 1),
            whole(vecs.shape),
            pl.BlockSpec((1, width, width), lambda i: (3, 0, 0)),
        ],
        out_specs=[rows_of(block, width), rows_of(block, width), rows_of(block, width), whole((8, width))],
        out_shape=[
            jax.ShapeDtypeStruct((rows, width), F32),
            jax.ShapeDtypeStruct((rows, width), BF),
            jax.ShapeDtypeStruct((rows, width), BF),
            jax.ShapeDtypeStruct((8, width), F32),
        ],
        compiler_params=params(),
        cost_estimate=cost(2 * rows * width * (hidden + width), 25e6),
        name="first_grad",
    )(inner, w_up, dz, norm_one, scale_one, vecs, w_qkvo)


def attention_backward_kernel(lengths, proj_ref, ctx_ref, lse_ref, out_ref, sum_ref):
    block, width = ctx_ref.shape
    step = pl.program_id(0)

    @pl.when(step == 0)
    def _():
        sum_ref[...] = jnp.zeros_like(sum_ref)

    masks = head_masks()
    lane = lax.broadcasted_iota(jnp.int32, (1, 2 * HD), 1)
    key = lax.broadcasted_iota(jnp.int32, (LEN, 1), 0)
    for seq in range(block // LEN):
        rows = slice(seq * LEN, (seq + 1) * LEN)
        valid = key < lengths[step * (block // LEN) + seq]
        for pair in range(width // (2 * HD)):
            at = pair * 2 * HD
            q = proj_ref[rows, at : at + 2 * HD] * BF(0.125)
            k = proj_ref[rows, width + at : width + at + 2 * HD]
            v = proj_ref[rows, 2 * width + at : 2 * width + at + 2 * HD]
            dctx = ctx_ref[rows, at : at + 2 * HD]
            keys = stack_heads(k, masks)
            scores = dot_nt(keys, q)
            dprobs = dot_nt(stack_heads(v, masks), dctx)
            probs, dscores = [], []
            for half in range(2):
                here = slice(half * LEN, (half + 1) * LEN)
                lse = lse_ref[seq, 2 * pair + half : 2 * pair + half + 1, :]
                prob = jnp.exp(jnp.where(valid, scores[here], -1e9) - lse)
                dprob = dprobs[here]
                inner = jnp.sum(prob * dprob, 0, keepdims=True)
                dscores.append((prob * (dprob - inner)).astype(BF))
                probs.append(prob.astype(BF))
            dv = dot_nn(jnp.concatenate(probs, axis=1), stack_heads(dctx, masks)).astype(BF)
            dk = dot_nn(jnp.concatenate(dscores, axis=1), stack_heads(q, masks)).astype(BF)
            dq = (dot_tn(jnp.concatenate(dscores, axis=0), keys) * 0.125).astype(BF)
            for offset, grad in ((0, dq), (width, dk), (2 * width, dv)):
                out_ref[rows, offset + at : offset + at + 2 * HD] = grad
                if offset != width:
                    sum_ref[0:1, offset + at : offset + at + 2 * HD] += jnp.sum(grad.astype(F32), 0, keepdims=True)


def attention_backward(lengths, proj, dctx, lse):
    rows, width = dctx.shape
    block = 2 * LEN
    return pl.pallas_call(
        attention_backward_kernel,
        grid_spec=pltpu.PrefetchScalarGridSpec(
            num_scalar_prefetch=1,
            grid=(rows // block,),
            in_specs=[
                rows_of(block, 3 * width),
                rows_of(block, width),
                pl.BlockSpec((block // LEN,) + lse.shape[1:], lambda i, *_: (i, 0, 0)),
            ],
            out_specs=[rows_of(block, 3 * width), whole((8, 3 * width))],
        ),
        out_shape=[jax.ShapeDtypeStruct((rows, 3 * width), BF), jax.ShapeDtypeStruct((8, 3 * width), F32)],
        compiler_params=params(),
        cost_estimate=cost(9e9, 12e6),
        name="attention_backward",
    )(lengths, proj, dctx, lse)


def input_grad_kernel(proj_ref, w_ref, dz_ref, out_ref):
    width = dz_ref.shape[1]
    grad = dz_ref[...]
    for unit in range(3):
        grad += dot_nt(proj_ref[:, unit * width : (unit + 1) * width], w_ref[unit])
    out_ref[...] = grad.astype(BF)


def input_grad(dproj, w_qkvo, dz, block=256):
    rows, width = dz.shape
    return pl.pallas_call(
        input_grad_kernel,
        grid=(rows // block,),
        in_specs=[rows_of(block, 3 * width), whole((3, width, width)), rows_of(block, width)],
        out_specs=rows_of(block, width),
        out_shape=jax.ShapeDtypeStruct((rows, width), BF),
        compiler_params=params(),
        cost_estimate=cost(6 * rows * width * width, 12e6),
        name="input_grad",
    )(dproj, w_qkvo, dz)


CORES = [(i, i ^ 1) for i in range(8)]


def from_core(value):
    return lax.ppermute(value, "shard", CORES)


def from_chip(value, ahead):
    return lax.ppermute(value, "shard", [((i + 2 * ahead) % 8, i) for i in range(8)])


def to_chip(value, ahead):
    return lax.ppermute(value, "shard", [(i, (i + 2 * ahead) % 8) for i in range(8)])


def from_rep(value, flip):
    return lax.ppermute(value, "rep", [(i, i ^ flip) for i in range(4)])


def joined(*parts):
    return jnp.concatenate(parts, 0)


def gather_units(place, own, direct, after=()):
    depth = own.shape[1]
    mine = lax.dynamic_index_in_dim(own, place[0], 0, keepdims=True)
    if after:
        mine = lax.optimization_barrier((mine,) + tuple(after))[0]
    hops = [from_chip(mine, ahead) for ahead in (1, 2, 3)]
    got = joined(*hops)
    pieces, plan = [own], [[(unit, False, 0, 0, 0, depth, depth) for unit in range(4)]]

    def entries(flips, first, count):
        return [(flip, True, 0, ahead, first, count, depth) for flip in flips for ahead in (1, 2, 3)]

    if direct:
        for flip in range(4):
            pieces.append(from_rep(got, flip) if flip else got)
            plan.append(entries((flip,), 0, depth))
    else:
        half = depth // 2
        low, high = got[:, :half], got[:, half:]
        low = joined(low, from_rep(low, 1))
        high = joined(high, from_rep(high, 2))
        pieces += [low, from_rep(low, 2), high, from_rep(high, 1)]
        plan += [entries((0, 1), 0, half), entries((2, 3), 0, half), entries((0, 2), half, half), entries((1, 3), half, half)]
    pieces += [from_core(piece) for piece in pieces]
    plan += [[entry[:2] + (1,) + entry[3:] for entry in listed] for listed in plan]
    return (plan, pieces), hops


def scatter_units(keep, send, order):
    one, two = order
    other = from_core(send).astype(F32)
    keep = keep.astype(F32) + other
    away = joined(keep[one : one + 1], keep[3:4]).astype(BF)
    got = from_rep(away, one).astype(F32)
    got = from_rep((keep[two] + got[1]).astype(BF), two).astype(F32) + (keep[0] + got[0])
    low = got.astype(BF)
    total = got[0]
    for ahead in (1, 2, 3):
        total = total + to_chip(low[ahead], ahead).astype(F32)
    return share_units(total.astype(BF)[None])


def share_units(own):
    pair = joined(own, from_rep(own, 1))
    return joined(pair, from_rep(pair, 2))


def natural_units(place, units):
    rep = place[0]
    units = jnp.where(rep & 1 == 1, units[jnp.array([1, 0, 3, 2])], units)
    return jnp.where(rep & 2 == 2, units[jnp.array([2, 3, 0, 1])], units)


def per_device(mesh_shape, *arrays):
    (tokens, cotangent, task, lengths, task_masks, w_qkv, qv_bias, w_out, out_bias, ln1_gain, ln1_bias, w_up, up_bias, w_down, down_bias, ln2_gain, ln2_bias) = arrays
    rows, width = tokens.shape
    shards = mesh_shape["shard"]
    hidden = up_bias.shape[0] * shards
    fast = shards == 8 and mesh_shape["rep"] == 4
    place = jnp.stack([lax.axis_index("rep"), lax.axis_index("shard") // 2, lax.axis_index("shard") % 2]).astype(jnp.int32)
    shard = lax.axis_index("shard")

    vectors = (qv_bias, out_bias, ln1_gain, ln1_bias, down_bias, ln2_gain, ln2_bias, up_bias)
    sizes = [v.shape[0] for v in vectors]
    packed = jnp.concatenate(vectors)

    if fast:
        depth = w_qkv.shape[0]
        own_a = jnp.concatenate([w_qkv.reshape(depth, 3, width), w_out.reshape(depth, 1, width)], 1).transpose(1, 0, 2)
        own_b = w_up.reshape(depth, 4, width).transpose(1, 0, 2)
        weight_a, hops = gather_units(place, own_a, True)
        packed_rows = jnp.pad(packed, (0, 16 * width - packed.shape[0])).reshape(1, 16, width)
        vec_rows = joined(packed_rows, *[from_chip(packed_rows, ahead) for ahead in (1, 2, 3)])
        vec_rows = jnp.stack([vec_rows, from_core(vec_rows)], 1).reshape(8, -1)[:, : packed.shape[0]]
        index = jnp.arange(8)
        slot = 2 * ((index // 2 - place[1]) % 4) + ((index % 2) ^ place[2])
        pick = (slot[:, None] == index[None, :]).astype(BF)
        all_vectors = jnp.dot(pick, vec_rows, preferred_element_type=F32)
        weight_b, hops_b = gather_units(place, own_b, False, hops)
        down_full = lax.all_gather(lax.optimization_barrier((w_down,) + tuple(hops))[0], "shard", axis=0, tiled=True)
    else:
        all_vectors = lax.all_gather(packed, "shard", axis=0).astype(F32)
        full_a = jnp.concatenate([lax.all_gather(w_qkv, "shard", axis=0, tiled=True), lax.all_gather(w_out, "shard", axis=0, tiled=True)], 1)
        full_b = lax.all_gather(w_up, "shard", axis=0, tiled=True)
        whole_plan = [[(unit, False, 0, 0, 0, width, 0) for unit in range(4)]]
        weight_a = (whole_plan, [full_a.reshape(width, 4, width).transpose(1, 0, 2)])
        weight_b = (whole_plan, [full_b.reshape(width, 4, width).transpose(1, 0, 2)])
        down_full = lax.all_gather(w_down, "shard", axis=0, tiled=True)

    full, start = [], 0
    for size in sizes:
        full.append(all_vectors[:, start : start + size].reshape(-1))
        start += size
    qv, out_shift, gain_one, shift_one, down_shift, gain_two, shift_two, up_shift = full
    qkv_shift = jnp.concatenate([qv[:width], jnp.zeros((width,), F32), qv[width:]])[None]
    vecs = jnp.stack([out_shift, gain_one, shift_one, down_shift, gain_two, shift_two, shift_two, shift_two])
    up_shift = up_shift[None]

    position = jnp.arange(LEN, dtype=jnp.int32)
    token_task = jnp.repeat(task, LEN)
    chosen = jnp.where(token_task == 0, task_masks[0], jnp.where(token_task == 1, task_masks[1], task_masks[2]))
    row_weight = chosen * (position[None, :] < lengths[:, None]).astype(jnp.int32).reshape(rows)
    row_weight = row_weight.astype(F32)[:, None]

    proj, context, lse, w_a = attention_forward(place, lengths, tokens, qkv_shift, weight_a)
    norm_one, scale_one, first_low, act, slope, w_b = middle(place, tokens, context, w_a, vecs, up_shift, weight_b)
    output, dz_two, dffn, sums_two = ffn_out(act, down_full, norm_one, cotangent, row_weight, vecs)
    grads_c = grad_down_natural(dffn, act, shards)
    dinner, sums_up = inner_grad(dffn, down_full, slope)
    grads_b = unit_grads(place, (first_low,), dinner, dffn, fast)
    dz_one, dattended, dcontext, sums_one = first_grad(dinner, w_b, dz_two, norm_one, scale_one, vecs, w_a)
    dproj, sums_qkv = attention_backward(lengths, proj, dcontext, lse)
    grads_a = unit_grads(place, (tokens, context), dproj, dattended, fast)
    grad_input = input_grad(dproj, w_a, dz_one)

    grad_vectors = (jnp.concatenate([sums_qkv[0, :width], sums_qkv[0, 2 * width :]]), sums_one[2], sums_one[0], sums_one[1], sums_two[2], sums_two[0], sums_two[1], sums_up[0])
    table = jnp.concatenate([g.reshape(shards, -1) for g in grad_vectors], 1)
    table = lax.psum(table, ("rep", "shard"))
    mine = lax.dynamic_index_in_dim(table, shard, 0, keepdims=False)
    final, start = [], 0
    for size in sizes:
        final.append(mine[start : start + size])
        start += size
    f_qv, f_out_shift, f_gain_one, f_shift_one, f_down_shift, f_gain_two, f_shift_two, f_up_shift = final

    final_c = lax.psum_scatter(grads_c, "shard", scatter_dimension=0, tiled=True)
    final_c = lax.psum(final_c.astype(BF), "rep").astype(F32)[0].T
    if fast:
        units_b = natural_units(place, scatter_units(*grads_b, (2, 1)))
        units_a = natural_units(place, scatter_units(*grads_a, (1, 2)))
    else:
        units = []
        for (grads,) in (grads_b, grads_a):
            summed = lax.psum_scatter(grads, "shard", scatter_dimension=1, tiled=True)
            units.append(lax.psum(summed.astype(BF), "rep"))
        units_b, units_a = units
    wide_b = units_b.astype(F32).transpose(1, 0, 2).reshape(-1, hidden)
    wide_a = units_a[:3].astype(F32).transpose(1, 0, 2).reshape(-1, 3 * width)
    return (output, grad_input, wide_a, f_qv, units_a[3].astype(F32), f_out_shift, f_gain_one, f_shift_one, wide_b, f_up_shift, final_c, f_down_shift, f_gain_two, f_shift_two)


def solution(mesh):
    split, shard = P(("rep", "shard"), None), P("shard")
    flat, matrix = P(("rep", "shard")), P("shard", None)
    in_specs = (split, split, flat, flat, P(None, ("rep", "shard")), matrix, shard, matrix, shard, shard, shard, matrix, shard, matrix, shard, shard, shard)
    out_specs = (split, split, matrix, shard, matrix, shard, shard, shard, matrix, shard, matrix, shard, shard, shard)
    return jax.shard_map(
        functools.partial(per_device, dict(mesh.shape)), mesh=mesh, in_specs=in_specs, out_specs=out_specs, check_vma=False
    )
```

time: 651 us -> 444 us (0.68); the launches traced: 640 us -> 443 us
  waiting for transfers between devices: 307 us -> 158 us
  matrix products: 145 us -> 0.19 us
  Pallas kernels: 0 us -> 138 us
  starting transfers between devices: 0.36 us -> 43.8 us
  blocking collectives: 80.7 us -> 40.9 us
  local copies, waits for them, and re-layouts: 60.4 us -> 29.5 us
  other arithmetic: 28.4 us -> 18.2 us
    reduce_scatter x3 -> x1, waiting for transfers between devices: 196 us -> 0.02 us  [per_device(): lax.psum_scatter(grads_c, 'shard', scatter_dimension=0, tiled=True)]
    dot_general x18 -> x1, matrix products: 145 us -> 0.19 us  [per_device(): all_vectors = jnp.dot(pick, vec_rows, preferred_element_type=F32)]
    pallas_call x0 -> x10, Pallas kernels: none -> 138 us  [the longest x1 29 us: middle(): pl.pallas_call(functools.partial(middle_kernel, plan), grid_spec=pltpu.Pr...]
    ppermute x0 -> x43, waiting for transfers between devices: none -> 115 us  [the longest x15 59.8 us: from_rep(): return lax.ppermute(value, 'rep', [(i, i ^ flip) for i in range(4)])]
    unnamed x2 -> x0, blocking collectives: 58 us -> none
    unnamed x10 -> x3, waiting for transfers between devices: 52.8 us -> 0.05 us
    all_gather x4 -> x1, waiting for transfers between devices: 43.9 us -> 0.02 us  [per_device(): lax.all_gather(lax.optimization_barrier((w_down,) + tuple(hops))[0], 'sha...]
    ppermute x0 -> x43, starting transfers between devices: none -> 43.7 us  [the longest x15 19.6 us: from_rep(): return lax.ppermute(value, 'rep', [(i, i ^ flip) for i in range(4)])]
  transfers between devices with their start and end apart: 9 -> 46, of which waited for: 6 -> 19; matrix products, arithmetic and copies ran while one was open for 26% -> 8% of each run, Pallas kernels for 0% -> 22%
where the time goes in v1:
time: 444 us; the launch traced here: 443 us
  waiting for transfers between devices  158 us (36%)
  Pallas kernels  138 us (31%)
  starting transfers between devices  43.8 us (10%)
  blocking collectives  40.9 us (9%)
  local copies, waits for them, and re-layouts  29.5 us (7%)
  other arithmetic  18.2 us (4%)
  between operations  14.6 us (3%)
    ppermute x15, waiting for transfers between devices, from_rep(): return lax.ppermute(value, 'rep', [(i, i ^ flip) for i in range(4)])  59.8 us
    psum x1, waiting for transfers between devices, per_device(): final_c = lax.psum(final_c.astype(BF), 'rep').astype(F32)[0].T  42.6 us
    ppermute x9, waiting for transfers between devices, from_chip(): lax.ppermute(value, 'shard', [((i + 2 * ahead) % 8, i) for i in range(8)])  41.4 us
    psum x1, blocking collectives, per_device(): table = lax.psum(table, ('rep', 'shard'))  40.9 us
    pallas_call x1, Pallas kernels, middle(): pl.pallas_call(functools.partial(middle_kernel, plan), grid_spec=pltpu.Pr...  29 us
    ppermute x15, starting transfers between devices, from_rep(): return lax.ppermute(value, 'rep', [(i, i ^ flip) for i in range(4)])  19.6 us
    pallas_call x2, Pallas kernels, unit_grads(): pl.pallas_call(functools.partial(unit_grads_kernel, len(lefts), relative)...  19.5 us
    pallas_call x1, Pallas kernels, attention_forward(): pl.pallas_call(functools.partial(attention_forward_kernel, plan), grid_sp...  18.2 us
  transfers between devices with their start and end apart: 46, of which 19 were waited for; matrix products, arithmetic and copies ran while one was open for 8% of the time, Pallas kernels for 22%

profile of v1, /device:TPU:0, one launch (start us, length us, event | category | flops | bytes accessed | tf_op | source)
XLA Modules:
  0.0 443.2 jit_solution(12796415516389181684)
XLA Ops:
  8.5 5.1 %collective-permute-start.4 = (bf16[1,96,768]{2,1,0:T(8,128)(2,1)S(1)}, bf16[1,96,768]{2,1,0:T(8,128)(2,1)S(1)}, u32[]{:S(2)}, u32[]{:S(2)}) collective-permute-start(bf16[1,96,768]{2,1,0:T(8,128)(2,1)S(1)} %fusion.20), channel_id=1, source_target_pairs={{2,0},{3,1},{4,2},{5,3},{6,4},{7,5},{0,6},{1,7},{10,8},{11,9},{12,... | collective-permute-start | bytes 442376 | tf_op jit(solution)/shard_map/ppermute | solution.py:540
  14.6 3.3 collective-permute-done.4
  17.9 8.2 %collective-permute-done.5 = bf16[1,96,768]{2,1,0:T(8,128)(2,1)S(1)} collective-permute-done((bf16[1,96,768]{2,1,0:T(8,128)(2,1)S(1)}, bf16[1,96,768]{2,1,0:T(8,128)(2,1)S(1)}, u32[]{:S(2)}, u32[]{:S(2)}) %collective-permute-start.5) | collective-permute-done | bytes 147488 | tf_op jit(solution)/shard_map/ppermute | solution.py:540
  26.1 5.5 %concatenate.56 = bf16[1152]{0:T(1024)(128)(2,1)S(1)} concatenate(bf16[192]{0:T(256)(128)(2,1)} %param.27, bf16[96]{0:T(256)(128)(2,1)} %param.29, bf16[96]{0:T(256)(128)(2,1)} %param.30, bf16[96]{0:T(256)(128)(2,1)} %param.31, bf16[96]{0:T(256)(128)(2,1)} %param.35, bf16[96]{0:T(256)(128)(2,1)} %param.36, bf16[96]{0:T(256)(128)(2,1)} %param.37, bf16[384]{0:T(512)(128)(2,1)} %param.33), dimensions={0} | concatenate | bytes 4608 | tf_op jit(solution)/shard_map/concatenate | solution.py:619
  31.7 1.5 collective-permute-start
  33.2 1.4 collective-permute-start.1
  34.6 1.9 collective-permute-start.2
  44.2 1.9 collective-permute-start.15
  46.9 9.5 %collective-permute-done.15 = bf16[1,96,768]{2,1,0:T(8,128)(2,1)S(1)} collective-permute-done((bf16[1,96,768]{2,1,0:T(8,128)(2,1)S(1)}, bf16[1,96,768]{2,1,0:T(8,128)(2,1)S(1)}, u32[]{:S(2)}, u32[]{:S(2)}) %collective-permute-start.15) | collective-permute-done | bytes 147488 | tf_op jit(solution)/shard_map/ppermute | solution.py:540
  56.4 20.4 %collective-permute-done.16 = bf16[1,96,768]{2,1,0:T(8,128)(2,1)S(1)} collective-permute-done((bf16[1,96,768]{2,1,0:T(8,128)(2,1)S(1)}, bf16[1,96,768]{2,1,0:T(8,128)(2,1)S(1)}, u32[]{:S(2)}, u32[]{:S(2)}) %collective-permute-start.16) | collective-permute-done | bytes 147488 | tf_op jit(solution)/shard_map/ppermute | solution.py:540
  76.9 1.5 collective-permute-start.20
  78.6 1.9 collective-permute-start.7
  81.1 4.1 collective-permute-done.20
  88.5 7.9 %collective-permute-done.7.refs_2_ = bf16[3,96,768]{2,1,0:T(8,128)(2,1)} collective-permute-done((bf16[3,96,768]{2,1,0:T(8,128)(2,1)S(1)}, bf16[3,96,768]{2,1,0:T(8,128)(2,1)}, u32[]{:S(2)}, u32[]{:S(2)}) %collective-permute-start.7) | collective-permute-done | bytes 442400 | tf_op jit(solution)/shard_map/ppermute | solution.py:548
  96.5 1.9 collective-permute-start.19
  98.4 7.5 %collective-permute-done.9.refs_4_ = bf16[3,96,768]{2,1,0:T(8,128)(2,1)} collective-permute-done((bf16[3,96,768]{2,1,0:T(8,128)(2,1)S(1)}, bf16[3,96,768]{2,1,0:T(8,128)(2,1)}, u32[]{:S(2)}, u32[]{:S(2)}) %collective-permute-start.9) | collective-permute-done | bytes 442400 | tf_op jit(solution)/shard_map/ppermute | solution.py:548
  107.1 7.2 %collective-permute-done.21.refs_4_ = bf16[6,48,768]{2,1,0:T(8,128)(2,1)} collective-permute-done((bf16[6,48,768]{2,1,0:T(8,128)(2,1)S(1)}, bf16[6,48,768]{2,1,0:T(8,128)(2,1)}, u32[]{:S(2)}, u32[]{:S(2)}) %collective-permute-start.21) | collective-permute-done | bytes 442400 | tf_op jit(solution)/shard_map/ppermute | solution.py:548
  115.4 18.2 %attention_forward.1 = (bf16[1024,2304]{1,0:T(8,128)(2,1)}, bf16[1024,768]{1,0:T(8,128)(2,1)}, f32[8,16,128]{2,1,0:T(8,128)S(1)}, bf16[4,768,768]{2,1,0:T(8,128)(2,1)}) custom-call(s32[3]{0:T(128)S(1)} %pad_add_fusion.place, s32[8]{0:T(128)S(1)} %copy-done.3, bf16[1024,768]{1,0:T(8,128)(2,1)} %refs_0_.1, f32[1,2304]{1,0:T(1,128)S(1)} %broadcast_in_dim.35.shift_ref, ...), custom_call_target="tpu_custom_call" | custom-call | flops 7247757312 | bytes 14000000 | tf_op jit(solution)/shard_map/attention_forward/pallas_call | solution.py:158
  133.6 29.0 %middle.1 = (f32[1024,768]{1,0:T(8,128)}, f32[1024,1]{1,0:T(8,128)S(1)}, bf16[1024,768]{1,0:T(8,128)(2,1)}, bf16[1024,3072]{1,0:T(8,128)(2,1)}, bf16[1024,3072]{...) custom-call(s32[3]{0:T(128)S(1)} %pad_add_fusion.place, bf16[1024,768]{1,0:T(8,128)(2,1)} %refs_0_.1, ...), custom_call_target="tpu_custom_call" | custom-call | flops 6039797760 | bytes 25000000 | tf_op jit(solution)/shard_map/middle/pallas_call | solution.py:211
  164.1 12.4 %ffn_out.1 = (bf16[1024,768]{1,0:T(8,128)(2,1)}, f32[1024,768]{1,0:T(8,128)}, bf16[1024,768]{1,0:T(8,128)(2,1)S(1)}, f32[8,768]{1,0:T(8,128)S(1)}) custom-call(bf16[1024,3072]{1,0:T(8,128)(2,1)} %get-tuple-element.45.act_ref, bf16[3072,768]{1,0:T(8,128)(2,1)} %all-gather.2.cloned.1.call-done.w_ref, f32[1024,768]{1,0:T(8,128)} %get-tuple-element.47.norm_ref, ...), custom_call_target="tpu_custom_call" | custom-call | flops 4831838208 | bytes 22000000 | tf_op jit(solution)/shard_map/ffn_out/pallas_call | solution.py:263
  176.5 9.0 %grad_down.1 = bf16[8,768,384]{2,1,0:T(8,128)(2,1)} custom-call(bf16[1024,768]{1,0:T(8,128)(2,1)S(1)} %get-tuple-element.50.low_ref.refs_2_, bf16[1024,3072]{1,0:T(8,128)(2,1)} %get-tuple-element.45.act_ref), custom_call_target="tpu_custom_call" | custom-call | flops 4831838208 | bytes 13000000 | tf_op jit(solution)/shard_map/grad_down/pallas_call | solution.py:303
  188.1 10.8 %inner_grad.1 = (bf16[1024,3072]{1,0:T(8,128)(2,1)}, f32[8,3072]{1,0:T(8,128)S(1)}) custom-call(bf16[1024,768]{1,0:T(8,128)(2,1)S(1)} %copy-done.5, bf16[3072,768]{1,0:T(8,128)(2,1)} %all-gather.2.cloned.1.call-done.w_ref, bf16[1024,3072]{1,0:T(8,128)(2,1)} %get-tuple-element.51.slope_ref), custom_call_target="tpu_custom_call" | custom-call | flops 4831838208 | bytes 18000000 | tf_op jit(solution)/shard_map/inner_grad/pallas_call | solution.py:333
  198.9 9.6 %unit_grads.3 = (bf16[4,4,96,768]{3,2,1,0:T(8,128)(2,1)S(1)}, bf16[4,4,96,768]{3,2,1,0:T(8,128)(2,1)}) custom-call(s32[3]{0:T(128)S(1)} %pad_add_fusion.place, bf16[1024,768]{1,0:T(8,128)(2,1)S(1)} %copy-done.8, bf16[1024,3072]{1,0:T(8,128)(2,1)} %get-tuple-element.52.inner_ref.refs_1_, bf16[1024,768]{1,0:T(8,128)(2,1)S(1)} %copy-done.6), custom_call_target="tpu_custom_call" | custom-call | flops 4831838208 | bytes 13000000 | tf_op jit(solution)/shard_map/unit_grads/pallas_call | solution.py:388
  209.0 15.5 %first_grad.1 = (f32[1024,768]{1,0:T(8,128)}, bf16[1024,768]{1,0:T(8,128)(2,1)S(1)}, bf16[1024,768]{1,0:T(8,128)(2,1)S(1)}, f32[8,768]{1,0:T(8,128)S(1)}) custom-call(bf16[1024,3072]{1,0:T(8,128)(2,1)} %get-tuple-element.52.inner_ref.refs_1_, bf16[4,768,768]{2,1,0:T(8,128)(2,1)} %get-tuple-element.53.w_ref, f32[1024,768]{1,0:T(8,128)} %get-tuple-element.54.dz_ref, ...), custom_call_target="tpu_custom_call" | custom-call | flops 6039797760 | bytes 25000000 | tf_op jit(solution)/shard_map/first_grad/pallas_call | solution.py:422
  224.5 16.0 %attention_backward.1 = (bf16[1024,2304]{1,0:T(8,128)(2,1)}, f32[8,2304]{1,0:T(8,128)S(1)}) custom-call(s32[8]{0:T(128)S(1)} %copy-done.3, bf16[1024,2304]{1,0:T(8,128)(2,1)} %get-tuple-element.49.proj_ref, bf16[1024,768]{1,0:T(8,128)(2,1)S(1)} %get-tuple-element.56.ctx_ref, f32[8,16,128]{2,1,0:T(8,128)S(1)} %get-tuple-element.57.lse_ref), custom_call_target="tpu_custom_call" | custom-call | flops 8999999488 | bytes 12000000 | tf_op jit(solution)/shard_map/attention_backward/pallas_call | solution.py:491
  240.6 9.9 %unit_grads.2 = (bf16[4,4,96,768]{3,2,1,0:T(8,128)(2,1)}, bf16[4,4,96,768]{3,2,1,0:T(8,128)(2,1)}) custom-call(s32[3]{0:T(128)S(1)} %pad_add_fusion.place, bf16[1024,768]{1,0:T(8,128)(2,1)S(1)} %copy-done.2, bf16[1024,768]{1,0:T(8,128)(2,1)S(1)} %copy-done.7, bf16[1024,2304]{1,0:T(8,128)(2,1)} %get-tuple-element.58.proj_ref.refs_2_, ...), custom_call_target="tpu_custom_call" | custom-call | flops 4831838208 | bytes 13000000 | tf_op jit(solution)/shard_map/unit_grads/pallas_call | solution.py:388
  250.5 2.2 convert_add_fusion
  256.2 2.5 convert_add_fusion.1
  262.8 8.0 %input_grad.1 = bf16[1024,768]{1,0:T(8,128)(2,1)} custom-call(bf16[1024,2304]{1,0:T(8,128)(2,1)} %get-tuple-element.58.proj_ref.refs_2_, bf16[4,768,768]{2,1,0:T(8,128)(2,1)} %get-tuple-element.43.w_out_ref.w_ref, f32[1024,768]{1,0:T(8,128)S(1)} %copy-done), custom_call_target="tpu_custom_call" | custom-call | flops 3623878656 | bytes 12000000 | tf_op jit(solution)/shard_map/input_grad/pallas_call | solution.py:520
  270.7 11.8 %collective-permute-done.36 = bf16[2,4,96,768]{3,2,1,0:T(8,128)(2,1)} collective-permute-done((bf16[2,4,96,768]{3,2,1,0:T(8,128)(2,1)}, bf16[2,4,96,768]{3,2,1,0:T(8,128)(2,1)}, u32[]{:S(2)}, u32[]{:S(2)}) %collective-permute-start.36) | collective-permute-done | bytes 1179680 | tf_op jit(solution)/shard_map/ppermute | solution.py:548
  282.6 1.5 convert_element_type.109
  286.2 2.8 collective-permute-done.28
  289.0 1.5 convert_element_type.96
  293.1 8.2 %collective-permute-done.37 = bf16[4,96,768]{2,1,0:T(8,128)(2,1)} collective-permute-done((bf16[4,96,768]{2,1,0:T(8,128)(2,1)}, bf16[4,96,768]{2,1,0:T(8,128)(2,1)}, u32[]{:S(2)}, u32[]{:S(2)}) %collective-permute-start.37) | collective-permute-done | bytes 589856 | tf_op jit(solution)/shard_map/ppermute | solution.py:548
  301.2 2.0 fusion.32
  304.7 2.8 collective-permute-start.40
  307.5 1.5 fusion.34
  309.3 1.5 collective-permute-start.31
  311.9 1.8 collective-permute-start.32
  313.7 4.6 %collective-permute-done.39 = bf16[96,768]{1,0:T(8,128)(2,1)S(1)} collective-permute-done((bf16[96,768]{1,0:T(8,128)(2,1)S(1)}, bf16[96,768]{1,0:T(8,128)(2,1)S(1)}, u32[]{:S(2)}, u32[]{:S(2)}) %collective-permute-start.39) | collective-permute-done | bytes 147488 | tf_op jit(solution)/shard_map/ppermute | solution.py:544
  318.4 4.1 collective-permute-start.41
  322.4 7.2 %collective-permute-done.31 = bf16[96,768]{1,0:T(8,128)(2,1)S(1)} collective-permute-done((bf16[96,768]{1,0:T(8,128)(2,1)S(1)}, bf16[96,768]{1,0:T(8,128)(2,1)S(1)}, u32[]{:S(2)}, u32[]{:S(2)}) %collective-permute-start.31) | collective-permute-done | bytes 147488 | tf_op jit(solution)/shard_map/ppermute | solution.py:544
  330.9 40.9 %psum.14 = f32[8,1152]{1,0:T(8,128)S(1)} all-reduce(f32[8,1152]{1,0:T(8,128)S(1)} %concatenate.70), channel_id=1, replica_groups=mesh['rep'=4,'shard'=8] {'rep','shard'}, use_global_device_ids=true, to_apply=%region_0.1 | all-reduce | flops 9216 | bytes 73728 | tf_op jit(solution)/shard_map/psum | solution.py:672
  371.8 2.3 collective-permute-start.42
  376.2 6.0 %collective-permute-done.42 = bf16[2,96,768]{2,1,0:T(8,128)(2,1)S(1)} collective-permute-done((bf16[2,96,768]{2,1,0:T(8,128)(2,1)S(1)}, bf16[2,96,768]{2,1,0:T(8,128)(2,1)S(1)}, u32[]{:S(2)}, u32[]{:S(2)}) %collective-permute-start.42) | collective-permute-done | bytes 294944 | tf_op jit(solution)/shard_map/ppermute | solution.py:548
  382.8 3.8 collective-permute-done.34
  391.7 42.6 %all-reduce.3.cloned.1.call-done = bf16[384,768]{0,1:T(8,128)(2,1)} async-done(((bf16[384,768]{0,1:T(8,128)(2,1)}), bf16[384,768]{0,1:T(8,128)(2,1)}) %all-reduce.3.cloned.1.call-update) | async-done | bytes 589840 | tf_op jit(solution)/shard_map/psum | solution.py:681
  434.4 2.3 copy.59
  (220 shorter events, 45.5 us)
Async XLA Ops:
  7.2 155.4 %all-gather.2.cloned.1.call-start = ((), (), s32[]{:S(2)}) async-start(), calls=%async_computation.1 | async-start | bytes 5308416 | tf_op jit(solution)/shard_map/all_gather | solution.py:634
  8.5 9.4 %collective-permute-start.4 = (bf16[1,96,768]{2,1,0:T(8,128)(2,1)S(1)}, bf16[1,96,768]{2,1,0:T(8,128)(2,1)S(1)}, u32[]{:S(2)}, u32[]{:S(2)}) collective-permute-start(bf16[1,96,768]{2,1,0:T(8,128)(2,1)S(1)} %fusion.20), channel_id=1, source_target_pairs={{2,0},{3,1},{4,2},{5,3},{6,4},{7,5},{0,6},{1,7},{10,8},{11,9},{12,... | collective-permute-start | bytes 442376 | tf_op jit(solution)/shard_map/ppermute | solution.py:540
  13.6 12.5 %collective-permute-start.5 = (bf16[1,96,768]{2,1,0:T(8,128)(2,1)S(1)}, bf16[1,96,768]{2,1,0:T(8,128)(2,1)S(1)}, u32[]{:S(2)}, u32[]{:S(2)}) collective-permute-start(bf16[1,96,768]{2,1,0:T(8,128)(2,1)S(1)} %fusion.20), channel_id=1, source_target_pairs={{4,0},{5,1},{6,2},{7,3},{0,4},{1,5},{2,6},{3,7},{12,8},{13,9},{14,... | collective-permute-start | bytes 442376 | tf_op jit(solution)/shard_map/ppermute | solution.py:540
  13.6 12.5 %collective-permute-start.6 = (bf16[1,96,768]{2,1,0:T(8,128)(2,1)S(1)}, bf16[1,96,768]{2,1,0:T(8,128)(2,1)S(1)}, u32[]{:S(2)}, u32[]{:S(2)}) collective-permute-start(bf16[1,96,768]{2,1,0:T(8,128)(2,1)S(1)} %fusion.20), channel_id=1, source_target_pairs={{6,0},{7,1},{0,2},{1,3},{2,4},{3,5},{4,6},{5,7},{14,8},{15,9},{8,1... | collective-permute-start | bytes 442376 | tf_op jit(solution)/shard_map/ppermute | solution.py:540
  26.1 362.6 %reduce-scatter.2.cloned.1.call-start = ((), (), s32[]{:S(2)}) async-start(), calls=%async_computation.2 | async-start | bytes 5308416 | tf_op jit(solution)/shard_map/reduce_scatter | solution.py:680
  31.7 10.1 %collective-permute-start = (bf16[1,16,768]{2,1,0:T(8,128)(2,1)S(1)}, bf16[1,16,768]{2,1,0:T(8,128)(2,1)}, u32[]{:S(2)}, u32[]{:S(2)}) collective-permute-start(bf16[1,16,768]{2,1,0:T(8,128)(2,1)S(1)} %reshape.195), channel_id=1, source_target_pairs={{2,0},{3,1},{4,2},{5,3},{6,4},{7,5},{0,6},{1,7},{10,8},{11,9},{12,... | collective-permute-start | bytes 73736 | tf_op jit(solution)/shard_map/ppermute | solution.py:540
  33.2 9.4 %collective-permute-start.1 = (bf16[1,16,768]{2,1,0:T(8,128)(2,1)S(1)}, bf16[1,16,768]{2,1,0:T(8,128)(2,1)S(1)}, u32[]{:S(2)}, u32[]{:S(2)}) collective-permute-start(bf16[1,16,768]{2,1,0:T(8,128)(2,1)S(1)} %reshape.195), channel_id=1, source_target_pairs={{4,0},{5,1},{6,2},{7,3},{0,4},{1,5},{2,6},{3,7},{12,8},{13,9},{14,... | collective-permute-start | bytes 73736 | tf_op jit(solution)/shard_map/ppermute | solution.py:540
  34.6 8.0 %collective-permute-start.2 = (bf16[1,16,768]{2,1,0:T(8,128)(2,1)S(1)}, bf16[1,16,768]{2,1,0:T(8,128)(2,1)S(1)}, u32[]{:S(2)}, u32[]{:S(2)}) collective-permute-start(bf16[1,16,768]{2,1,0:T(8,128)(2,1)S(1)} %reshape.195), channel_id=1, source_target_pairs={{6,0},{7,1},{0,2},{1,3},{2,4},{3,5},{4,6},{5,7},{14,8},{15,9},{8,1... | collective-permute-start | bytes 73736 | tf_op jit(solution)/shard_map/ppermute | solution.py:540
  36.6 69.8 %collective-permute-start.10 = (bf16[4,96,768]{2,1,0:T(8,128)(2,1)S(1)}, bf16[4,96,768]{2,1,0:T(8,128)(2,1)}, u32[]{:S(2)}, u32[]{:S(2)}) collective-permute-start(bf16[4,96,768]{2,1,0:T(8,128)(2,1)S(1)} %fusion.6.refs_0_), channel_id=1, source_target_pairs={{0,1},{1,0},{2,3},{3,2},{4,5},{5,4},{6,7},{7,6},{8,9},{9,8},{10,11... | collective-permute-start | bytes 1769480 | tf_op jit(solution)/shard_map/ppermute | solution.py:536
  41.7 36.9 %copy-start.17 = (bf16[1,96,768]{2,1,0:T(8,128)(2,1)S(1)}, bf16[1,96,768]{2,1,0:T(8,128)(2,1)}, u32[]{:S(2)}) copy-start(bf16[1,96,768]{2,1,0:T(8,128)(2,1)} %copy-done.16) | copy-start | bytes 442372
  41.7 36.9 %copy-start.19 = (bf16[1,96,768]{2,1,0:T(8,128)(2,1)S(1)}, bf16[1,96,768]{2,1,0:T(8,128)(2,1)}, u32[]{:S(2)}) copy-start(bf16[1,96,768]{2,1,0:T(8,128)(2,1)} %copy-done.18) | copy-start | bytes 442372
  42.6 1.5 collective-permute-start.3
  44.2 12.3 %collective-permute-start.15 = (bf16[1,96,768]{2,1,0:T(8,128)(2,1)S(1)}, bf16[1,96,768]{2,1,0:T(8,128)(2,1)S(1)}, u32[]{:S(2)}, u32[]{:S(2)}) collective-permute-start(bf16[1,96,768]{2,1,0:T(8,128)(2,1)S(1)} %bitcast.161), channel_id=1, source_target_pairs={{2,0},{3,1},{4,2},{5,3},{6,4},{7,5},{0,6},{1,7},{10,8},{11,9},{12,... | collective-permute-start | bytes 442376 | tf_op jit(solution)/shard_map/ppermute | solution.py:540
  46.3 30.5 %collective-permute-start.16 = (bf16[1,96,768]{2,1,0:T(8,128)(2,1)S(1)}, bf16[1,96,768]{2,1,0:T(8,128)(2,1)S(1)}, u32[]{:S(2)}, u32[]{:S(2)}) collective-permute-start(bf16[1,96,768]{2,1,0:T(8,128)(2,1)S(1)} %bitcast.162), channel_id=1, source_target_pairs={{4,0},{5,1},{6,2},{7,3},{0,4},{1,5},{2,6},{3,7},{12,8},{13,9},{14,... | collective-permute-start | bytes 442376 | tf_op jit(solution)/shard_map/ppermute | solution.py:540
  46.3 30.5 %collective-permute-start.17 = (bf16[1,96,768]{2,1,0:T(8,128)(2,1)S(1)}, bf16[1,96,768]{2,1,0:T(8,128)(2,1)S(1)}, u32[]{:S(2)}, u32[]{:S(2)}) collective-permute-start(bf16[1,96,768]{2,1,0:T(8,128)(2,1)S(1)} %bitcast.163), channel_id=1, source_target_pairs={{6,0},{7,1},{0,2},{1,3},{2,4},{3,5},{4,6},{5,7},{14,8},{15,9},{8,1... | collective-permute-start | bytes 442376 | tf_op jit(solution)/shard_map/ppermute | solution.py:540
  76.9 8.3 %collective-permute-start.20 = (bf16[3,48,768]{2,1,0:T(8,128)(2,1)S(1)}, bf16[3,48,768]{2,1,0:T(8,128)(2,1)S(1)}, u32[]{:S(2)}, u32[]{:S(2)}) collective-permute-start(bf16[3,48,768]{2,1,0:T(8,128)(2,1)S(1)} %get-tuple-element.134), channel_id=1, source_target_pairs={{0,16},{8,24},{16,0},{24,8},{1,17},{9,25},{17,1},{25,9},{2,18},{10... | collective-permute-start | bytes 663560 | tf_op jit(solution)/shard_map/ppermute | solution.py:548
  78.4 8.3 %collective-permute-start.18 = (bf16[3,48,768]{2,1,0:T(8,128)(2,1)S(1)}, bf16[3,48,768]{2,1,0:T(8,128)(2,1)S(1)}, u32[]{:S(2)}, u32[]{:S(2)}) collective-permute-start(bf16[3,48,768]{2,1,0:T(8,128)(2,1)S(1)} %get-tuple-element.135), channel_id=1, source_target_pairs={{0,8},{8,0},{16,24},{24,16},{1,9},{9,1},{17,25},{25,17},{2,10},{10... | collective-permute-start | bytes 663560 | tf_op jit(solution)/shard_map/ppermute | solution.py:548
  78.6 17.7 %collective-permute-start.7 = (bf16[3,96,768]{2,1,0:T(8,128)(2,1)S(1)}, bf16[3,96,768]{2,1,0:T(8,128)(2,1)}, u32[]{:S(2)}, u32[]{:S(2)}) collective-permute-start(bf16[3,96,768]{2,1,0:T(8,128)(2,1)S(1)} %constant_dynamic-update-slice_fusion.4.refs_1_), channel_id=1, source_target_pairs={{0,8},{8,0},{16,24},{24,16},{1,9},{9,1},{17,25},{25,17},{2,10},{10... | collective-permute-start | bytes 1327112 | tf_op jit(solution)/shard_map/ppermute | solution.py:548
  80.6 15.9 %collective-permute-start.8 = (bf16[3,96,768]{2,1,0:T(8,128)(2,1)S(1)}, bf16[3,96,768]{2,1,0:T(8,128)(2,1)}, u32[]{:S(2)}, u32[]{:S(2)}) collective-permute-start(bf16[3,96,768]{2,1,0:T(8,128)(2,1)S(1)} %constant_dynamic-update-slice_fusion.4.refs_1_), channel_id=1, source_target_pairs={{0,16},{8,24},{16,0},{24,8},{1,17},{9,25},{17,1},{25,9},{2,18},{10... | collective-permute-start | bytes 1327112 | tf_op jit(solution)/shard_map/ppermute | solution.py:548
  85.2 20.6 %collective-permute-start.9 = (bf16[3,96,768]{2,1,0:T(8,128)(2,1)S(1)}, bf16[3,96,768]{2,1,0:T(8,128)(2,1)}, u32[]{:S(2)}, u32[]{:S(2)}) collective-permute-start(bf16[3,96,768]{2,1,0:T(8,128)(2,1)S(1)} %constant_dynamic-update-slice_fusion.4.refs_1_), channel_id=1, source_target_pairs={{0,24},{8,16},{16,8},{24,0},{1,25},{9,17},{17,9},{25,1},{2,26},{10... | collective-permute-start | bytes 1327112 | tf_op jit(solution)/shard_map/ppermute | solution.py:548
  86.7 19.1 %collective-permute-start.11 = (bf16[3,96,768]{2,1,0:T(8,128)(2,1)S(1)}, bf16[3,96,768]{2,1,0:T(8,128)(2,1)}, u32[]{:S(2)}, u32[]{:S(2)}) collective-permute-start(bf16[3,96,768]{2,1,0:T(8,128)(2,1)S(1)} %constant_dynamic-update-slice_fusion.4.refs_1_), channel_id=1, source_target_pairs={{0,1},{1,0},{2,3},{3,2},{4,5},{5,4},{6,7},{7,6},{8,9},{9,8},{10,11... | collective-permute-start | bytes 1327112 | tf_op jit(solution)/shard_map/ppermute | solution.py:536
  96.3 18.0 %collective-permute-start.21 = (bf16[6,48,768]{2,1,0:T(8,128)(2,1)S(1)}, bf16[6,48,768]{2,1,0:T(8,128)(2,1)}, u32[]{:S(2)}, u32[]{:S(2)}) collective-permute-start(bf16[6,48,768]{2,1,0:T(8,128)(2,1)S(1)} %pad_maximum_fusion.5.refs_3_), channel_id=1, source_target_pairs={{0,8},{8,0},{16,24},{24,16},{1,9},{9,1},{17,25},{25,17},{2,10},{10... | collective-permute-start | bytes 1327112 | tf_op jit(solution)/shard_map/ppermute | solution.py:548
  96.5 17.9 %collective-permute-start.19 = (bf16[6,48,768]{2,1,0:T(8,128)(2,1)S(1)}, bf16[6,48,768]{2,1,0:T(8,128)(2,1)}, u32[]{:S(2)}, u32[]{:S(2)}) collective-permute-start(bf16[6,48,768]{2,1,0:T(8,128)(2,1)S(1)} %pad_maximum_fusion.4.refs_1_), channel_id=1, source_target_pairs={{0,16},{8,24},{16,0},{24,8},{1,17},{9,25},{17,1},{25,9},{2,18},{10... | collective-permute-start | bytes 1327112 | tf_op jit(solution)/shard_map/ppermute | solution.py:548
  105.8 9.0 %collective-permute-start.12 = (bf16[3,96,768]{2,1,0:T(8,128)(2,1)}, bf16[3,96,768]{2,1,0:T(8,128)(2,1)}, u32[]{:S(2)}, u32[]{:S(2)}) collective-permute-start(bf16[3,96,768]{2,1,0:T(8,128)(2,1)} %collective-permute-done.7.refs_2_), channel_id=1, source_target_pairs={{0,1},{1,0},{2,3},{3,2},{4,5},{5,4},{6,7},{7,6},{8,9},{9,8},{10,11... | collective-permute-start | bytes 1327112 | tf_op jit(solution)/shard_map/ppermute | solution.py:536
  105.8 9.1 %collective-permute-start.13 = (bf16[3,96,768]{2,1,0:T(8,128)(2,1)}, bf16[3,96,768]{2,1,0:T(8,128)(2,1)}, u32[]{:S(2)}, u32[]{:S(2)}) collective-permute-start(bf16[3,96,768]{2,1,0:T(8,128)(2,1)} %collective-permute-done.8.refs_3_), channel_id=1, source_target_pairs={{0,1},{1,0},{2,3},{3,2},{4,5},{5,4},{6,7},{7,6},{8,9},{9,8},{10,11... | collective-permute-start | bytes 1327112 | tf_op jit(solution)/shard_map/ppermute | solution.py:536
  106.4 9.0 %collective-permute-start.14 = (bf16[3,96,768]{2,1,0:T(8,128)(2,1)}, bf16[3,96,768]{2,1,0:T(8,128)(2,1)}, u32[]{:S(2)}, u32[]{:S(2)}) collective-permute-start(bf16[3,96,768]{2,1,0:T(8,128)(2,1)} %collective-permute-done.9.refs_4_), channel_id=1, source_target_pairs={{0,1},{1,0},{2,3},{3,2},{4,5},{5,4},{6,7},{7,6},{8,9},{9,8},{10,11... | collective-permute-start | bytes 1327112 | tf_op jit(solution)/shard_map/ppermute | solution.py:536
  114.3 19.3 %collective-permute-start.22 = (bf16[4,96,768]{2,1,0:T(8,128)(2,1)S(1)}, bf16[4,96,768]{2,1,0:T(8,128)(2,1)S(1)}, u32[]{:S(2)}, u32[]{:S(2)}) collective-permute-start(bf16[4,96,768]{2,1,0:T(8,128)(2,1)S(1)} %bitcast.146), channel_id=1, source_target_pairs={{0,1},{1,0},{2,3},{3,2},{4,5},{5,4},{6,7},{7,6},{8,9},{9,8},{10,11... | collective-permute-start | bytes 1769480 | tf_op jit(solution)/shard_map/ppermute | solution.py:536
  114.3 19.3 %collective-permute-start.25 = (bf16[6,48,768]{2,1,0:T(8,128)(2,1)S(1)}, bf16[6,48,768]{2,1,0:T(8,128)(2,1)S(1)}, u32[]{:S(2)}, u32[]{:S(2)}) collective-permute-start(bf16[6,48,768]{2,1,0:T(8,128)(2,1)S(1)} %pad_maximum_fusion.5.refs_3_), channel_id=1, source_target_pairs={{0,1},{1,0},{2,3},{3,2},{4,5},{5,4},{6,7},{7,6},{8,9},{9,8},{10,11... | collective-permute-start | bytes 1327112 | tf_op jit(solution)/shard_map/ppermute | solution.py:536
  114.8 18.8 %collective-permute-start.23 = (bf16[6,48,768]{2,1,0:T(8,128)(2,1)S(1)}, bf16[6,48,768]{2,1,0:T(8,128)(2,1)S(1)}, u32[]{:S(2)}, u32[]{:S(2)}) collective-permute-start(bf16[6,48,768]{2,1,0:T(8,128)(2,1)S(1)} %pad_maximum_fusion.4.refs_1_), channel_id=1, source_target_pairs={{0,1},{1,0},{2,3},{3,2},{4,5},{5,4},{6,7},{7,6},{8,9},{9,8},{10,11... | collective-permute-start | bytes 1327112 | tf_op jit(solution)/shard_map/ppermute | solution.py:536
  114.9 18.7 %collective-permute-start.26 = (bf16[6,48,768]{2,1,0:T(8,128)(2,1)}, bf16[6,48,768]{2,1,0:T(8,128)(2,1)S(1)}, u32[]{:S(2)}, u32[]{:S(2)}) collective-permute-start(bf16[6,48,768]{2,1,0:T(8,128)(2,1)} %collective-permute-done.21.refs_4_), channel_id=1, source_target_pairs={{0,1},{1,0},{2,3},{3,2},{4,5},{5,4},{6,7},{7,6},{8,9},{9,8},{10,11... | collective-permute-start | bytes 1327112 | tf_op jit(solution)/shard_map/ppermute | solution.py:536
  115.3 18.3 %collective-permute-start.24 = (bf16[6,48,768]{2,1,0:T(8,128)(2,1)}, bf16[6,48,768]{2,1,0:T(8,128)(2,1)S(1)}, u32[]{:S(2)}, u32[]{:S(2)}) collective-permute-start(bf16[6,48,768]{2,1,0:T(8,128)(2,1)} %collective-permute-done.19.refs_2_), channel_id=1, source_target_pairs={{0,1},{1,0},{2,3},{3,2},{4,5},{5,4},{6,7},{7,6},{8,9},{9,8},{10,11... | collective-permute-start | bytes 1327112 | tf_op jit(solution)/shard_map/ppermute | solution.py:536
  208.5 42.1 %collective-permute-start.35 = (bf16[4,4,96,768]{3,2,1,0:T(8,128)(2,1)}, bf16[4,4,96,768]{3,2,1,0:T(8,128)(2,1)}, u32[]{:S(2)}, u32[]{:S(2)}) collective-permute-start(bf16[4,4,96,768]{3,2,1,0:T(8,128)(2,1)} %get-tuple-element.69), channel_id=1, source_target_pairs={{0,1},{1,0},{2,3},{3,2},{4,5},{5,4},{6,7},{7,6},{8,9},{9,8},{10,11... | collective-permute-start | bytes 7077896 | tf_op jit(solution)/shard_map/ppermute | solution.py:536
  208.9 225.4 %all-reduce.3.cloned.1.call-start = ((), (), s32[]{:S(2)}) async-start(), calls=%async_computation.3 | async-start | bytes 1179648 | tf_op jit(solution)/shard_map/psum | solution.py:681
  250.5 4.9 %collective-permute-start.27 = (bf16[4,4,96,768]{3,2,1,0:T(8,128)(2,1)}, bf16[4,4,96,768]{3,2,1,0:T(8,128)(2,1)}, u32[]{:S(2)}, u32[]{:S(2)}) collective-permute-start(bf16[4,4,96,768]{3,2,1,0:T(8,128)(2,1)} %get-tuple-element.62), channel_id=1, source_target_pairs={{0,1},{1,0},{2,3},{3,2},{4,5},{5,4},{6,7},{7,6},{8,9},{9,8},{10,11... | collective-permute-start | bytes 7077896 | tf_op jit(solution)/shard_map/ppermute | solution.py:536
  254.0 28.6 %collective-permute-start.36 = (bf16[2,4,96,768]{3,2,1,0:T(8,128)(2,1)}, bf16[2,4,96,768]{3,2,1,0:T(8,128)(2,1)}, u32[]{:S(2)}, u32[]{:S(2)}) collective-permute-start(bf16[2,4,96,768]{3,2,1,0:T(8,128)(2,1)} %concatenate.76), channel_id=1, source_target_pairs={{0,16},{8,24},{16,0},{24,8},{1,17},{9,25},{17,1},{25,9},{2,18},{10... | collective-permute-start | bytes 3538952 | tf_op jit(solution)/shard_map/ppermute | solution.py:548
  260.0 29.1 %collective-permute-start.28 = (bf16[2,4,96,768]{3,2,1,0:T(8,128)(2,1)}, bf16[2,4,96,768]{3,2,1,0:T(8,128)(2,1)}, u32[]{:S(2)}, u32[]{:S(2)}) collective-permute-start(bf16[2,4,96,768]{3,2,1,0:T(8,128)(2,1)} %pad_maximum_fusion), channel_id=1, source_target_pairs={{0,8},{8,0},{16,24},{24,16},{1,9},{9,1},{17,25},{25,17},{2,10},{10... | collective-permute-start | bytes 3538952 | tf_op jit(solution)/shard_map/ppermute | solution.py:548
  285.1 16.1 %collective-permute-start.37 = (bf16[4,96,768]{2,1,0:T(8,128)(2,1)}, bf16[4,96,768]{2,1,0:T(8,128)(2,1)}, u32[]{:S(2)}, u32[]{:S(2)}) collective-permute-start(bf16[4,96,768]{2,1,0:T(8,128)(2,1)} %fusion.8), channel_id=1, source_target_pairs={{0,8},{8,0},{16,24},{24,16},{1,9},{9,1},{17,25},{25,17},{2,10},{10... | collective-permute-start | bytes 1769480 | tf_op jit(solution)/shard_map/ppermute | solution.py:548
  291.5 16.0 %collective-permute-start.29 = (bf16[4,96,768]{2,1,0:T(8,128)(2,1)}, bf16[4,96,768]{2,1,0:T(8,128)(2,1)S(1)}, u32[]{:S(2)}, u32[]{:S(2)}) collective-permute-start(bf16[4,96,768]{2,1,0:T(8,128)(2,1)} %fusion.7), channel_id=1, source_target_pairs={{0,16},{8,24},{16,0},{24,8},{1,17},{9,25},{17,1},{25,9},{2,18},{10... | collective-permute-start | bytes 1769480 | tf_op jit(solution)/shard_map/ppermute | solution.py:548
  303.2 8.7 %collective-permute-start.38 = (bf16[96,768]{1,0:T(8,128)(2,1)S(1)}, bf16[96,768]{1,0:T(8,128)(2,1)S(1)}, u32[]{:S(2)}, u32[]{:S(2)}) collective-permute-start(bf16[96,768]{1,0:T(8,128)(2,1)S(1)} %get-tuple-element.128), channel_id=1, source_target_pairs={{0,2},{1,3},{2,4},{3,5},{4,6},{5,7},{6,0},{7,1},{8,10},{9,11},{10,... | collective-permute-start | bytes 442376 | tf_op jit(solution)/shard_map/ppermute | solution.py:544
  303.3 15.0 %collective-permute-start.39 = (bf16[96,768]{1,0:T(8,128)(2,1)S(1)}, bf16[96,768]{1,0:T(8,128)(2,1)S(1)}, u32[]{:S(2)}, u32[]{:S(2)}) collective-permute-start(bf16[96,768]{1,0:T(8,128)(2,1)S(1)} %get-tuple-element.130), channel_id=1, source_target_pairs={{0,4},{1,5},{2,6},{3,7},{4,0},{5,1},{6,2},{7,3},{8,12},{9,13},{10,... | collective-permute-start | bytes 442376 | tf_op jit(solution)/shard_map/ppermute | solution.py:544
  304.7 13.6 %collective-permute-start.40 = (bf16[96,768]{1,0:T(8,128)(2,1)S(1)}, bf16[96,768]{1,0:T(8,128)(2,1)S(1)}, u32[]{:S(2)}, u32[]{:S(2)}) collective-permute-start(bf16[96,768]{1,0:T(8,128)(2,1)S(1)} %get-tuple-element.129), channel_id=1, source_target_pairs={{0,6},{1,7},{2,0},{3,1},{4,2},{5,3},{6,4},{7,5},{8,14},{9,15},{10,... | collective-permute-start | bytes 442376 | tf_op jit(solution)/shard_map/ppermute | solution.py:544
  309.1 13.3 %collective-permute-start.30 = (bf16[96,768]{1,0:T(8,128)(2,1)S(1)}, bf16[96,768]{1,0:T(8,128)(2,1)S(1)}, u32[]{:S(2)}, u32[]{:S(2)}) collective-permute-start(bf16[96,768]{1,0:T(8,128)(2,1)S(1)} %get-tuple-element.131), channel_id=1, source_target_pairs={{0,2},{1,3},{2,4},{3,5},{4,6},{5,7},{6,0},{7,1},{8,10},{9,11},{10,... | collective-permute-start | bytes 442376 | tf_op jit(solution)/shard_map/ppermute | solution.py:544
  309.3 20.3 %collective-permute-start.31 = (bf16[96,768]{1,0:T(8,128)(2,1)S(1)}, bf16[96,768]{1,0:T(8,128)(2,1)S(1)}, u32[]{:S(2)}, u32[]{:S(2)}) collective-permute-start(bf16[96,768]{1,0:T(8,128)(2,1)S(1)} %get-tuple-element.133), channel_id=1, source_target_pairs={{0,4},{1,5},{2,6},{3,7},{4,0},{5,1},{6,2},{7,3},{8,12},{9,13},{10,... | collective-permute-start | bytes 442376 | tf_op jit(solution)/shard_map/ppermute | solution.py:544
  311.9 17.7 %collective-permute-start.32 = (bf16[96,768]{1,0:T(8,128)(2,1)S(1)}, bf16[96,768]{1,0:T(8,128)(2,1)S(1)}, u32[]{:S(2)}, u32[]{:S(2)}) collective-permute-start(bf16[96,768]{1,0:T(8,128)(2,1)S(1)} %get-tuple-element.132), channel_id=1, source_target_pairs={{0,6},{1,7},{2,0},{3,1},{4,2},{5,3},{6,4},{7,5},{8,14},{9,15},{10,... | collective-permute-start | bytes 442376 | tf_op jit(solution)/shard_map/ppermute | solution.py:544
  318.4 53.4 %collective-permute-start.41 = (bf16[1,96,768]{2,1,0:T(8,128)(2,1)S(1)}, bf16[1,96,768]{2,1,0:T(8,128)(2,1)S(1)}, u32[]{:S(2)}, u32[]{:S(2)}) collective-permute-start(bf16[1,96,768]{2,1,0:T(8,128)(2,1)S(1)} %fusion.18), channel_id=1, source_target_pairs={{0,8},{8,0},{16,24},{24,16},{1,9},{9,1},{17,25},{25,17},{2,10},{10... | collective-permute-start | bytes 442376 | tf_op jit(solution)/shard_map/ppermute | solution.py:548
  329.7 44.5 %collective-permute-start.33 = (bf16[1,96,768]{2,1,0:T(8,128)(2,1)S(1)}, bf16[1,96,768]{2,1,0:T(8,128)(2,1)S(1)}, u32[]{:S(2)}, u32[]{:S(2)}) collective-permute-start(bf16[1,96,768]{2,1,0:T(8,128)(2,1)S(1)} %fusion.17), channel_id=1, source_target_pairs={{0,8},{8,0},{16,24},{24,16},{1,9},{9,1},{17,25},{25,17},{2,10},{10... | collective-permute-start | bytes 442376 | tf_op jit(solution)/shard_map/ppermute | solution.py:548
  371.8 10.3 %collective-permute-start.42 = (bf16[2,96,768]{2,1,0:T(8,128)(2,1)S(1)}, bf16[2,96,768]{2,1,0:T(8,128)(2,1)S(1)}, u32[]{:S(2)}, u32[]{:S(2)}) collective-permute-start(bf16[2,96,768]{2,1,0:T(8,128)(2,1)S(1)} %pad_maximum_fusion.7), channel_id=1, source_target_pairs={{0,16},{8,24},{16,0},{24,8},{1,17},{9,25},{17,1},{25,9},{2,18},{10... | collective-permute-start | bytes 884744 | tf_op jit(solution)/shard_map/ppermute | solution.py:548
  374.2 12.4 %collective-permute-start.34 = (bf16[2,96,768]{2,1,0:T(8,128)(2,1)S(1)}, bf16[2,96,768]{2,1,0:T(8,128)(2,1)S(1)}, u32[]{:S(2)}, u32[]{:S(2)}) collective-permute-start(bf16[2,96,768]{2,1,0:T(8,128)(2,1)S(1)} %pad_maximum_fusion.6), channel_id=1, source_target_pairs={{0,16},{8,24},{16,0},{24,8},{1,17},{9,25},{17,1},{25,9},{2,18},{10... | collective-permute-start | bytes 884744 | tf_op jit(solution)/shard_map/ppermute | solution.py:548
  (24 other events, 335.4 us)
Sparse Core Ops, SparseCore 0:
  26.2 65.7 all-gather.1
  209.1 53.5 reduce-scatter.1
  388.9 45.4 all-reduce.2
